TPU v7x, 512 devices: a whole 4x8x8 slice. The times are simulated.
512 devices in a mesh: group: 16 (over z, core), dom: 32 (over x, y).
Axes of the slice: x: 4, y: 8, z: 8, core: 2. Of those that a mesh axis runs over, the one named last changes fastest.
Arguments:
- features: bfloat16 [196608, 512], P(('group', 'dom')), may hold values from -6 to 6
- w_self: bfloat16 [512, 512], replicated, may hold values from -0.25 to 0.25
- w_neigh: bfloat16 [512, 512], replicated, may hold values from -0.25 to 0.25
- bias_term: float32 [512], replicated, may hold values from -3 to 3
- degree: int32 [196608], P(('group', 'dom')), may hold values from 4 to 32
- local_adj: int32 [196608, 384], P(('group', 'dom')), may hold values 0 or 1
- hub_adj: int32 [196608, 512], P(('group', 'dom')), may hold values 0 or 1
- hub_rows: int32 [512, 1], P(('group', 'dom')), may hold values from 0 to 383
- remote_adj: int32 [196608, 256], P(('group', 'dom')), may hold values 0 or 1
- send_rows: int32 [512, 32, 8], P(('group', 'dom')), may hold values from 0 to 383
- send_counts: int32 [512, 32], P(('group', 'dom')), may hold values from 0 to 8, as said below
- grad_out: bfloat16 [196608, 512], P(('group', 'dom')), may hold values from -6 to 6
Outputs:
- out_feats: bfloat16 [196608, 512], P(('group', 'dom'))
- grad_features: bfloat16 [196608, 512], P(('group', 'dom'))
- hub_grad: float32 [512, 512], P(('group', 'dom'))
Inputs may be any that keep to these rules, and one draw needn't show every extreme that they name: send_counts[p, j] live slots are the first ones of send_rows[p, j]; a device sends nothing to itself (entry j equal to its own index along dom is 0); in every group some device receives 8 live rows from every other device of the group. send_rows[p, j, s] is a local row of device p; rows may repeat. Hub number p * 1 + k is local row hub_rows[p, k] of device p.
All inputs are finite; a program needn't handle non-finite values. No bound on the sum of `local_adj` or of `hub_adj` or of `remote_adj` on one device may be relied on, other than what follows from the above.
Results may differ from a plain program's by a relative error of at most 0.014.
Values may be sent and summed in bfloat16 or wider, within the bound.
No kernel may reach another device: no remote copies, remote signals or barrier semaphores. Data moves between devices by JAX's collectives and lax.ppermute only.
A program may use at most 64 MiB of HBM per device.

v0:
```python
import jax
import jax.numpy as jnp
from jax import lax
from jax.sharding import PartitionSpec as P


def transposed(matrix, other):
    return lax.dot_general(
        matrix, other, (((0,), (0,)), ((), ())), preferred_element_type=jnp.float32
    )


def back_product(grads, weight):
    return lax.dot_general(
        grads, weight, (((1,), (1,)), ((), ())), preferred_element_type=jnp.float32
    )


def on_device(
    features,
    w_self,
    w_neigh,
    bias_term,
    degree,
    local_adj,
    hub_adj,
    hub_rows,
    remote_adj,
    send_rows,
    send_counts,
    grad_out,
):
    node_count = features.shape[0]
    feat_width = features.shape[1]
    peer_count = lax.axis_size("dom")
    slot_count = send_rows.shape[2]
    hub_mat = hub_adj.astype(jnp.bfloat16)
    local_mat = local_adj.astype(jnp.bfloat16)
    remote_mat = remote_adj.astype(jnp.bfloat16)
    live_slots = jnp.arange(slot_count, dtype=jnp.int32)[None, :] < send_counts[0][:, None]
    outgoing = jnp.where(
        live_slots[:, :, None], features[send_rows[0]], jnp.zeros((), jnp.bfloat16)
    )
    incoming = lax.all_to_all(outgoing, "dom", split_axis=0, concat_axis=0, tiled=True)
    received = incoming.reshape(peer_count * slot_count, feat_width)
    hub_own = features[hub_rows[0]]
    all_hubs = lax.all_gather(hub_own, ("group", "dom"), axis=0, tiled=True)
    hub_sum = jnp.dot(hub_mat, all_hubs, preferred_element_type=jnp.float32)
    summed = features.astype(jnp.float32) + jnp.dot(
        local_mat, features, preferred_element_type=jnp.float32
    )
    summed = summed + hub_sum + jnp.dot(remote_mat, received, preferred_element_type=jnp.float32)
    denom = degree.astype(jnp.float32)[:, None] + 1.0
    mean_feats = (summed / denom).astype(jnp.bfloat16)
    preact = jnp.dot(features, w_self, preferred_element_type=jnp.float32)
    preact = preact + jnp.dot(mean_feats, w_neigh, preferred_element_type=jnp.float32) + bias_term
    out_feats = jax.nn.elu(preact).astype(jnp.bfloat16)
    slope = jnp.where(preact > 0, 1.0, jnp.exp(jnp.minimum(preact, 0.0)))
    grad_pre = (grad_out.astype(jnp.float32) * slope).astype(jnp.bfloat16)
    back_self = back_product(grad_pre, w_self)
    grad_mean = (back_product(grad_pre, w_neigh) / denom).astype(jnp.bfloat16)
    slot_grad = transposed(remote_mat, grad_mean).astype(jnp.bfloat16)
    returned = lax.all_to_all(
        slot_grad.reshape(peer_count, slot_count, feat_width),
        "dom",
        split_axis=0,
        concat_axis=0,
        tiled=True,
    )
    hub_grad = lax.psum_scatter(
        transposed(hub_mat, grad_mean), ("group", "dom"), scatter_dimension=0, tiled=True
    )
    grad_local = back_self + grad_mean.astype(jnp.float32) + transposed(local_mat, grad_mean)
    returned = jnp.where(live_slots[:, :, None], returned, jnp.zeros((), jnp.bfloat16))
    node_index = jnp.arange(node_count, dtype=jnp.int32)[:, None]
    pick_rows = (send_rows[0].reshape(1, -1) == node_index).astype(jnp.bfloat16)
    back_add = jnp.dot(
        pick_rows, returned.reshape(-1, feat_width), preferred_element_type=jnp.float32
    )
    hub_pick = (hub_rows[0][None, :] == node_index).astype(jnp.float32)
    hub_add = jnp.dot(hub_pick, hub_grad, precision=lax.Precision.HIGHEST)
    grad_features = (grad_local + back_add + hub_add).astype(jnp.bfloat16)
    return (out_feats, grad_features, hub_grad)


def solution(mesh):
    placed = (
        P(("group", "dom"), None),
        P(),
        P(),
        P(),
        P(("group", "dom")),
        P(("group", "dom"), None),
        P(("group", "dom"), None),
        P(("group", "dom"), None),
        P(("group", "dom"), None),
        P(("group", "dom"), None, None),
        P(("group", "dom"), None),
        P(("group", "dom"), None),
    )
    return jax.shard_map(
        on_device,
        mesh=mesh,
        in_specs=placed,
        out_specs=(P(("group", "dom"), None), P(("group", "dom"), None), P(("group", "dom"), None)),
        check_vma=False,
    )
```

profile of v0, /device:TPU:24, one launch (start us, length us, event | category | flops | bytes accessed | tf_op | source)
XLA Modules:
  0.0 470.8 jit_solution(12204000386947432386)
XLA Ops:
  7.2 0.0 copy-start
  7.2 0.0 copy-start.8
  7.2 0.0 copy-start.6
  7.2 0.7 copy-done.8
  7.9 0.1 iota_compare_fusion.2
  8.0 0.0 copy-done.6
  8.0 0.1 copy.22
  8.1 0.1 reshape.125
  8.2 2.3 gather_fusion
  10.4 0.0 copy-start.3
  10.4 0.8 bitcast_select_fusion
  11.2 0.0 copy-start.1
  11.2 10.1 %all-to-all-start = ((bf16[32,8,512]{2,1,0:T(8,128)(2,1)}), bf16[32,8,512]{2,1,0:T(8,128)(2,1)S(1)}, u32[]{:S(2)}, u32[]{:S(2)}) async-start(bf16[32,8,512]{2,1,0:T(8,128)(2,1)} %bitcast_select_fusion), calls=%async_computation | async-start | bytes 524288 | tf_op jit(solution)/shard_map/all_to_all | solution.py:44
  22.0 0.0 copy-done.1
  22.0 0.0 copy-done.3
  22.0 1.3 fusion.43
  23.3 0.0 copy-start.2
  23.3 142.2 %all-gather = bf16[512,1,512]{2,1,0:T(2,128)(2,1)} all-gather(bf16[1,1,512]{2,1,0:T(2,128)(2,1)S(1)} %dynamic-slice_bitcast_fusion), channel_id=1, replica_groups=mesh['group'=16,'dom'=32] {'group','dom'}, dimensions={0}, use_global_device_ids=true | all-gather | bytes 525312 | tf_op jit(solution)/shard_map/all_gather | solution.py:47
  165.4 0.1 copy.25
  165.5 0.1 eq.41
  165.6 0.0 copy-start.7
  165.7 0.7 copy-done.7
  166.3 0.0 copy-done.2
  166.3 0.0 copy-start.4
  166.3 1.3 convolution_add_fusion
  167.6 0.0 copy-start.9
  167.6 0.0 all-to-all-done
  167.6 0.0 copy-done.4
  167.6 1.2 convolution_bitcast_fusion.3
  168.8 0.0 copy-done
  168.8 0.0 copy-done.9
  168.8 0.0 copy-start.5
  168.8 4.1 fusion.12
  172.9 0.0 copy-done.5
  172.9 1.5 fusion.7
  174.4 1.0 fusion.10
  175.5 7.9 %all-to-all-start.1 = ((bf16[32,8,512]{2,1,0:T(8,128)(2,1)}), bf16[32,8,512]{2,1,0:T(8,128)(2,1)S(1)}, u32[]{:S(2)}, u32[]{:S(2)}) async-start(bf16[32,8,512]{2,1,0:T(8,128)(2,1)} %fusion.10), calls=%async_computation.1 | async-start | bytes 524288 | tf_op jit(solution)/shard_map/all_to_all | solution.py:63
  183.4 0.0 all-reduce.3.cloned.1.call-start
  183.5 2.6 convolution_bitcast_fusion
  186.1 0.0 all-reduce.3.cloned.1.call-update
  186.1 1.6 convolution_add_fusion.1
  187.8 5.3 %all-to-all-done.1 = bf16[32,8,512]{2,1,0:T(8,128)(2,1)S(1)} async-done(((bf16[32,8,512]{2,1,0:T(8,128)(2,1)}), bf16[32,8,512]{2,1,0:T(8,128)(2,1)S(1)}, u32[]{:S(2)}, u32[]{:S(2)}) %all-to-all-start.1) | async-done | bytes 262176 | tf_op jit(solution)/shard_map/all_to_all | solution.py:63
  193.1 0.3 fusion.20
  193.5 267.5 %all-reduce.3.cloned.1.call-done = f32[512,512]{0,1:T(8,128)} async-done(((f32[512,512]{0,1:T(8,128)}), f32[512,512]{0,1:T(8,128)}) %all-reduce.3.cloned.1.call-update) | async-done | bytes 1048592
  460.9 1.2 fusion.38
  462.1 0.7 copy.26
  462.8 1.2 fusion.9
  (5 shorter events, 0.0 us)
Async XLA Ops:
  7.2 161.6 %copy-start = (bf16[512,512]{1,0:T(8,128)(2,1)S(1)}, bf16[512,512]{1,0:T(8,128)(2,1)}, u32[]{:S(2)}) copy-start(bf16[512,512]{1,0:T(8,128)(2,1)} %param.14) | copy-start | bytes 1572868
  7.2 0.7 copy-start.8
  7.2 0.8 copy-start.6
  10.4 11.6 %copy-start.3 = (bf16[512,512]{1,0:T(8,128)(2,1)S(1)}, bf16[512,512]{1,0:T(8,128)(2,1)}, u32[]{:S(2)}) copy-start(bf16[512,512]{1,0:T(8,128)(2,1)} %param.13) | copy-start | bytes 1572868
  11.2 10.7 %copy-start.1 = (bf16[384,512]{1,0:T(8,128)(2,1)S(1)}, bf16[384,512]{1,0:T(8,128)(2,1)}, u32[]{:S(2)}) copy-start(bf16[384,512]{1,0:T(8,128)(2,1)} %param.12) | copy-start | bytes 1179652
  11.2 156.3 %all-to-all-start = ((bf16[32,8,512]{2,1,0:T(8,128)(2,1)}), bf16[32,8,512]{2,1,0:T(8,128)(2,1)S(1)}, u32[]{:S(2)}, u32[]{:S(2)}) async-start(bf16[32,8,512]{2,1,0:T(8,128)(2,1)} %bitcast_select_fusion), calls=%async_computation | async-start | bytes 524288 | tf_op jit(solution)/shard_map/all_to_all | solution.py:44
  23.3 143.0 %copy-start.2 = (s32[384,384]{1,0:T(8,128)S(1)}, s32[384,384]{1,0:T(8,128)}, u32[]{:S(2)}) copy-start(s32[384,384]{1,0:T(8,128)} %param.17) | copy-start | bytes 1769476
  165.6 0.7 copy-start.7
  166.3 1.3 copy-start.4
  167.6 1.2 copy-start.9
  168.8 4.1 copy-start.5
  175.5 17.6 %all-to-all-start.1 = ((bf16[32,8,512]{2,1,0:T(8,128)(2,1)}), bf16[32,8,512]{2,1,0:T(8,128)(2,1)S(1)}, u32[]{:S(2)}, u32[]{:S(2)}) async-start(bf16[32,8,512]{2,1,0:T(8,128)(2,1)} %fusion.10), calls=%async_computation.1 | async-start | bytes 524288 | tf_op jit(solution)/shard_map/all_to_all | solution.py:63
  183.4 277.5 %all-reduce.3.cloned.1.call-start = ((), (), s32[]{:S(2)}) async-start(), calls=%async_computation.2 | async-start | bytes 2097152
Sparse Core Ops, SparseCore 0:
  189.3 271.5 all-reduce.2
where the time goes:
time: 471 us
  waiting for transfers between devices  273 us (58%)
  blocking collectives  142 us (30%)
  starting transfers between devices  18 us (4%)
  matrix products  16.2 us (3%)
  between operations  14.8 us (3%)
  local copies, waits for them, and re-layouts  5.87 us (1%)
    unnamed x2, waiting for transfers between devices  267 us
    all_gather x1, blocking collectives, on_device(): all_hubs = lax.all_gather(hub_own, ('group', 'dom'), axis=0, tiled=True)  142 us
    all_to_all x1, starting transfers between devices, on_device(): lax.all_to_all(outgoing, 'dom', split_axis=0, concat_axis=0, tiled=True)  10.1 us
  transfers between devices with their start and end apart: 3, of which 2 were waited for; matrix products, arithmetic and copies ran while one was open for 2% of the time, Pallas kernels for 0%

commit v1 on v0

v1 whole, which is shorter than its diff:
```python
import jax
import jax.numpy as jnp
from jax import lax
from jax.sharding import Mesh
from jax.sharding import PartitionSpec as P

ALL = ("z", "core", "x", "y")
DOM = ("x", "y")
F32 = jnp.float32
BF16 = jnp.bfloat16


def matmul(lhs, rhs):
    return jnp.dot(lhs, rhs, preferred_element_type=F32)


def transposed(matrix, other):
    return lax.dot_general(matrix, other, (((0,), (0,)), ((), ())), preferred_element_type=F32)


def back_product(grads, weight):
    return lax.dot_general(grads, weight, (((1,), (1,)), ((), ())), preferred_element_type=F32)


def exchange(parts, axis):
    return lax.all_to_all(parts, axis, split_axis=0, concat_axis=0, tiled=True)


def on_device(
    features,
    w_self,
    w_neigh,
    bias_term,
    degree,
    local_adj,
    hub_adj,
    hub_rows,
    remote_adj,
    send_rows,
    send_counts,
    grad_out,
):
    nodes, width = features.shape
    n_z, n_core = lax.axis_size("z"), lax.axis_size("core")
    peers, slots = send_rows.shape[1:]
    hubs = hub_adj.shape[1]
    half = hubs // n_core
    my_core = lax.axis_index("core")

    hub_own = lax.dynamic_slice(features, (hub_rows[0, 0], 0), (1, width)).reshape(1, width // 128, 128)
    along_z = exchange(jnp.broadcast_to(hub_own, (n_z, width // 128, 128)), "z").reshape(n_z, width)

    live = jnp.arange(slots, dtype=jnp.int32)[None, :] < send_counts[0][:, None]
    picked = jnp.where(live, send_rows[0], -1).reshape(1, peers * slots)
    pick = (picked == jnp.arange(nodes, dtype=jnp.int32)[:, None]).astype(BF16)
    outgoing = transposed(pick, features).astype(BF16).reshape(peers, slots, width)
    payload = jnp.concatenate([outgoing, jnp.broadcast_to(along_z[None], (peers, n_z, width))], axis=1)
    incoming = exchange(payload, DOM)
    received = incoming[:, :slots].reshape(peers * slots, width)
    same_core = incoming[:, slots:].reshape(half, width)
    all_hubs = lax.all_gather(same_core, "core", axis=0, tiled=True)

    place = jnp.arange(hubs, dtype=jnp.int32)[None, :]
    at_core, at_peer, at_z = place // half, (place % half) // n_z, place % n_z
    source = (at_z * n_core + at_core) * peers + at_peer
    reorder = (source == jnp.arange(hubs, dtype=jnp.int32)[:, None]).astype(BF16)
    hub_mat = matmul(hub_adj.astype(BF16), reorder).astype(BF16)
    local_mat = local_adj.astype(BF16)
    remote_mat = remote_adj.astype(BF16)

    summed = features.astype(F32) + matmul(local_mat, features)
    summed = summed + matmul(hub_mat, all_hubs) + matmul(remote_mat, received)
    denom = degree.astype(F32)[:, None] + 1.0
    mean_feats = (summed / denom).astype(BF16)
    preact = matmul(features, w_self) + matmul(mean_feats, w_neigh) + bias_term
    low = jnp.minimum(preact, 0.0)
    out_feats = jnp.where(preact > 0, preact, jnp.expm1(low)).astype(BF16)
    slope = jnp.where(preact > 0, 1.0, jnp.exp(low))
    grad_pre = (grad_out.astype(F32) * slope).astype(BF16)
    grad_mean = (back_product(grad_pre, w_neigh) / denom).astype(BF16)

    hub_low, hub_high = hub_mat[:, :half], hub_mat[:, half:]
    mine = jnp.where(my_core == 0, hub_low, hub_high)
    other = jnp.where(my_core == 0, hub_high, hub_low)
    other_part = lax.ppermute(transposed(other, grad_mean).astype(BF16), "core", [(0, 1), (1, 0)])
    chip_part = (transposed(mine, grad_mean) + other_part.astype(F32)).astype(BF16)
    slot_grad = transposed(remote_mat, grad_mean).astype(BF16)
    payload = jnp.concatenate(
        [slot_grad.reshape(peers, slots, width), chip_part.reshape(peers, n_z, width)], axis=1
    )
    returned = exchange(payload, DOM)
    hub_z = jnp.sum(returned[:, slots:].astype(F32), axis=0)
    hub_parts = exchange(hub_z.reshape(n_z, width // 128, 128), "z")
    hub_grad = jnp.sum(hub_parts, axis=0).reshape(1, width)

    grad_local = back_product(grad_pre, w_self) + grad_mean.astype(F32) + transposed(local_mat, grad_mean)
    grad_local = grad_local + matmul(pick, returned[:, :slots].reshape(peers * slots, width))
    at_hub = jnp.arange(nodes, dtype=jnp.int32)[:, None] == hub_rows[0, 0]
    grad_features = (grad_local + jnp.where(at_hub, hub_grad, 0.0)).astype(BF16)
    return (out_feats, grad_features, hub_grad)


def solution(mesh):
    fine = Mesh(mesh.devices.reshape(8, 2, 4, 8), ALL)
    rows, whole = P(ALL), P()
    return jax.shard_map(
        on_device,
        mesh=fine,
        in_specs=(rows, whole, whole, whole, rows, rows, rows, rows, rows, rows, rows, rows),
        out_specs=(rows, rows, rows),
        check_vma=False,
    )
```

time: 471 us -> 98.7 us (0.21)
  the two profiles are of different devices: /device:TPU:24 before, /device:TPU:8 now
where the time goes in v1:
time: 98.7 us; the launch traced here: 98 us
  waiting for transfers between devices  40.8 us (41%)
  starting transfers between devices  31 us (31%)
  matrix products  16.5 us (17%)
  local copies, waits for them, and re-layouts  3.75 us (4%)
  blocking collectives  2.45 us (2%)
  other arithmetic  1.94 us (2%)
  between operations  1.53 us (2%)
    all_to_all x4, waiting for transfers between devices, exchange(): return lax.all_to_all(parts, axis, split_axis=0, concat_axis=0, tiled=True)  39.8 us
    all_to_all x4, starting transfers between devices, exchange(): return lax.all_to_all(parts, axis, split_axis=0, concat_axis=0, tiled=True)  28.9 us
    dot_general x6, matrix products, matmul(): return jnp.dot(lhs, rhs, preferred_element_type=F32)  9.74 us
    dot_general x5, matrix products, transposed(): lax.dot_general(matrix, other, (((0,), (0,)), ((), ())), preferred_elemen...  3.44 us
    dot_general x2, matrix products, back_product(): lax.dot_general(grads, weight, (((1,), (1,)), ((), ())), preferred_elemen...  3.33 us
    all_gather x1, blocking collectives, on_device(): all_hubs = lax.all_gather(same_core, 'core', axis=0, tiled=True)  2.45 us
    ppermute x1, starting transfers between devices, on_device(): lax.ppermute(transposed(other, grad_mean).astype(BF16), 'core', [(0, 1),...  2.04 us
  transfers between devices with their start and end apart: 5, of which 5 were waited for; matrix products, arithmetic and copies ran while one was open for 9% of the time, Pallas kernels for 0%

profile of v1, /device:TPU:8, one launch (start us, length us, event | category | flops | bytes accessed | tf_op | source)
XLA Modules:
  0.0 98.0 jit_solution(1660379573638966819)
XLA Ops:
  0.6 0.0 copy-start
  1.4 0.7 dynamic-slice_reduce_fusion
  2.1 0.6 broadcast_in_dim.51
  2.7 0.0 copy-start.10
  2.7 10.4 %all-to-all-start = ((bf16[8,4,128]{2,1,0:T(4,128)(2,1)}), bf16[8,4,128]{2,1,0:T(4,128)(2,1)S(1)}, u32[]{:S(2)}, u32[]{:S(2)}) async-start(bf16[8,4,128]{2,1,0:T(4,128)(2,1)} %broadcast_in_dim.51), calls=%async_computation | async-start | bytes 16384 | tf_op jit(solution)/shard_map/all_to_all | solution.py:26
  13.1 0.0 copy-done.10
  13.1 0.1 copy.18
  13.2 0.1 squeeze.7
  13.3 0.0 copy-start.12
  13.3 0.6 copy-done.12
  14.0 0.1 iota_compare_fusion.4
  14.0 0.1 lt.41
  14.1 1.3 %fusion.9 = bf16[32,8,512]{2,1,0:T(8,128)(2,1)S(1)} fusion(bf16[384,512]{1,0:T(8,128)(2,1)} %param.12, s32[256]{0:T(256)S(1)} %broadcast_select_fusion), kind=kOutput, calls=%fused_computation.20 | convolution fusion | flops 100892672 | bytes 656384 | tf_op jit(solution)/shard_map/dot_general | solution.py:18
  15.5 5.4 %all-to-all-done = bf16[8,4,128]{2,1,0:T(4,128)(2,1)S(1)} async-done(((bf16[8,4,128]{2,1,0:T(4,128)(2,1)}), bf16[8,4,128]{2,1,0:T(4,128)(2,1)S(1)}, u32[]{:S(2)}, u32[]{:S(2)}) %all-to-all-start) | async-done | bytes 8224 | tf_op jit(solution)/shard_map/all_to_all | solution.py:26
  20.9 0.9 pad_maximum_fusion
  21.8 0.0 copy-start.7
  21.8 10.3 %all-to-all-start.1 = ((bf16[32,16,512]{2,1,0:T(8,128)(2,1)}), bf16[32,16,512]{2,1,0:T(8,128)(2,1)S(1)}, u32[]{:S(2)}, u32[]{:S(2)}) async-start(bf16[32,16,512]{2,1,0:T(8,128)(2,1)} %pad_maximum_fusion), calls=%async_computation.1 | async-start | bytes 1048576 | tf_op jit(solution)/shard_map/all_to_all | solution.py:26
  32.1 0.0 copy-start.11
  32.1 0.7 copy-done.11
  32.8 0.0 copy-done.7
  32.8 0.0 copy-start.1
  32.8 0.0 copy-start.4
  32.8 1.2 %convolution_convert_fusion = bf16[512,384]{1,0:T(8,128)(2,1)} fusion(s32[512]{0:T(512)S(1)} %fusion.48, s32[384,512]{1,0:T(8,128)S(1)} %copy-done.7), kind=kOutput, calls=%fused_computation.16 | convolution fusion | flops 202244096 | bytes 1181696 | tf_op jit(solution)/shard_map/dot_general | solution.py:14
  34.0 0.0 copy-done.1
  34.0 0.0 copy-done.4
  34.0 0.0 copy-start.2
  34.0 1.3 %fusion.58 = f32[384,512]{1,0:T(8,128)} fusion(bf16[384,512]{1,0:T(8,128)(2,1)S(1)} %copy-done.1, bf16[512,512]{1,0:T(8,128)(2,1)S(1)} %copy-done.4), kind=kOutput, calls=%fused_computation.91 | convolution fusion | flops 201326592 | bytes 1703936 | tf_op jit(solution)/shard_map/dot_general | solution.py:14
  35.3 0.0 copy-done.2
  35.3 1.3 %convolution_add_fusion = f32[384,512]{1,0:T(8,128)} fusion(bf16[384,512]{1,0:T(8,128)(2,1)S(1)} %copy-done.1, s32[384,384]{1,0:T(8,128)S(1)} %copy-done.2), kind=kOutput, calls=%fused_computation | convolution fusion | flops 151535616 | bytes 1769472 | tf_op jit(solution)/shard_map/dot_general | solution.py:14
  36.6 11.7 %all-to-all-done.1 = bf16[32,16,512]{2,1,0:T(8,128)(2,1)S(1)} async-done(((bf16[32,16,512]{2,1,0:T(8,128)(2,1)}), bf16[32,16,512]{2,1,0:T(8,128)(2,1)S(1)}, u32[]{:S(2)}, u32[]{:S(2)}) %all-to-all-start.1) | async-done | bytes 524320 | tf_op jit(solution)/shard_map/all_to_all | solution.py:26
  48.3 0.0 copy-start.5
  48.3 2.4 %all_gather.3 = bf16[512,512]{1,0:T(8,128)(2,1)} all-gather(bf16[256,512]{1,0:T(8,128)(2,1)S(1)} %slice_bitcast_fusion.4), channel_id=1, replica_groups=mesh['z'=8,'core'=2,'x'=4,'y'=8] {'core'}, dimensions={0}, use_global_device_ids=true | all-gather | bytes 786432 | tf_op jit(solution)/shard_map/all_gather | solution.py:61
  50.8 0.0 copy-done.5
  50.8 0.0 copy-start.6
  50.8 0.0 copy-start.13
  50.8 1.2 %convolution_bitcast_fusion.1 = f32[384,512]{1,0:T(8,128)} fusion(bf16[32,16,512]{2,1,0:T(8,128)(2,1)S(1)} %all-to-all-done.1, s32[384,256]{1,0:T(8,128)S(1)} %copy-done.5), kind=kOutput, calls=%fused_computation.12 | convolution fusion | flops 100761600 | bytes 1441792 | tf_op jit(solution)/shard_map/dot_general | solution.py:14
  52.0 0.0 copy-done
  52.0 0.0 copy-done.6
  52.0 0.0 copy-done.13
  52.0 3.6 %fusion.12 = (bf16[384,512]{1,0:T(8,128)(2,1)}, f32[384,512]{1,0:T(8,128)}) fusion(f32[512]{0:T(512)S(1)} %copy-done.13, f32[384,512]{1,0:T(8,128)} %fusion.58, bf16[512,512]{1,0:T(8,128)(2,1)S(1)} %copy-done, f32[384,512]{1,0:T(8,128)} %convolution_bitcast_fusion.1, f32[384,512]{1,0:T(8,128)S(1)} %copy-done.6, ...), kind=kOutput, calls=%fused_computation.26 | convolution fusion | flops 404619264 | bytes 4984320 | tf_op jit(solution)/shard_map/dot_general | solution.py:14
  55.5 0.0 copy-start.8
  55.5 1.7 %fusion.6 = bf16[384,512]{1,0:T(8,128)(2,1)S(1)} fusion(bf16[512,512]{1,0:T(8,128)(2,1)S(1)} %copy-done, f32[384]{0:T(512)S(1)} %convert_add_fusion, f32[384,512]{1,0:T(8,128)} %get-tuple-element.4, bf16[384,512]{1,0:T(8,128)(2,1)} %param.23), kind=kOutput, calls=%fused_computation.13 | convolution fusion | flops 202899456 | bytes 2098688 | tf_op jit(solution)/shard_map/dot_general | solution.py:22
  57.2 0.0 copy-done.8
  57.2 0.3 convolution_convert_fusion.1
  57.5 2.0 %collective-permute-start = (bf16[256,512]{1,0:T(8,128)(2,1)S(1)}, bf16[256,512]{1,0:T(8,128)(2,1)S(1)}, u32[]{:S(2)}, u32[]{:S(2)}) collective-permute-start(bf16[256,512]{1,0:T(8,128)(2,1)S(1)} %convolution_convert_fusion.1), channel_id=1, source_target_pairs={{0,32},{32,0},{1,33},{33,1},{2,34},{34,2},{3,35},{35,3},{4,36},{36... | collective-permute-start | bytes 786440 | tf_op jit(solution)/shard_map/ppermute | solution.py:85
  59.6 0.3 fusion.10
  59.9 1.0 %collective-permute-done = bf16[256,512]{1,0:T(8,128)(2,1)S(1)} collective-permute-done((bf16[256,512]{1,0:T(8,128)(2,1)S(1)}, bf16[256,512]{1,0:T(8,128)(2,1)S(1)}, u32[]{:S(2)}, u32[]{:S(2)}) %collective-permute-start) | collective-permute-done | bytes 262176 | tf_op jit(solution)/shard_map/ppermute | solution.py:85
  61.0 0.3 fusion.20
  61.3 0.9 pad_maximum_fusion.1
  62.2 4.8 %all-to-all-start.2 = ((bf16[32,16,512]{2,1,0:T(8,128)(2,1)}), bf16[32,16,512]{2,1,0:T(8,128)(2,1)S(1)}, u32[]{:S(2)}, u32[]{:S(2)}) async-start(bf16[32,16,512]{2,1,0:T(8,128)(2,1)} %pad_maximum_fusion.1), calls=%async_computation.2 | async-start | bytes 1048576 | tf_op jit(solution)/shard_map/all_to_all | solution.py:26
  67.0 1.6 %convolution_add_fusion.1 = f32[384,512]{1,0:T(8,128)S(1)} fusion(bf16[512,512]{1,0:T(8,128)(2,1)S(1)} %copy-done.4, bf16[384,512]{1,0:T(8,128)(2,1)S(1)} %fusion.6, f32[384,512]{1,0:T(8,128)} %get-tuple-element.4, bf16[384,512]{1,0:T(8,128)(2,1)} %param.23), kind=kOutput, calls=%fused_computation.4 | convolution fusion | flops 202899456 | bytes 2883584 | tf_op jit(solution)/shard_map/dot_general | solution.py:22
  68.7 16.3 %all-to-all-done.2 = bf16[32,16,512]{2,1,0:T(8,128)(2,1)S(1)} async-done(((bf16[32,16,512]{2,1,0:T(8,128)(2,1)}), bf16[32,16,512]{2,1,0:T(8,128)(2,1)S(1)}, u32[]{:S(2)}, u32[]{:S(2)}) %all-to-all-start.2) | async-done | bytes 524320 | tf_op jit(solution)/shard_map/all_to_all | solution.py:26
  84.9 0.0 copy-start.3
  85.0 0.7 reshape.175
  85.7 0.0 copy-done.3
  85.7 3.3 %all-to-all-start.3 = ((f32[8,4,128]{2,1,0:T(4,128)}), f32[8,4,128]{2,1,0:T(4,128)S(1)}, u32[]{:S(2)}, u32[]{:S(2)}) async-start(f32[8,4,128]{2,1,0:T(4,128)} %reshape.175), calls=%async_computation.3 | async-start | bytes 32768 | tf_op jit(solution)/shard_map/all_to_all | solution.py:26
  89.1 1.2 %fusion.18 = f32[384,512]{1,0:T(8,128)S(1)} fusion(bf16[32,16,512]{2,1,0:T(8,128)(2,1)} %copy-done.3, s32[256]{0:T(256)S(1)} %broadcast_select_fusion), kind=kOutput, calls=%fused_computation.36 | convolution fusion | flops 100761600 | bytes 1049600 | tf_op jit(solution)/shard_map/dot_general | solution.py:14
  90.3 6.5 %all-to-all-done.3 = f32[8,4,128]{2,1,0:T(4,128)S(1)} async-done(((f32[8,4,128]{2,1,0:T(4,128)}), f32[8,4,128]{2,1,0:T(4,128)S(1)}, u32[]{:S(2)}, u32[]{:S(2)}) %all-to-all-start.3) | async-done | bytes 16416 | tf_op jit(solution)/shard_map/all_to_all | solution.py:26
  96.8 0.0 copy-start.9
  96.8 1.2 %fusion.7 = bf16[384,512]{1,0:T(8,128)(2,1)} fusion(f32[384,512]{1,0:T(8,128)S(1)} %fusion.18, f32[384,512]{1,0:T(8,128)S(1)} %convolution_add_fusion.1, bf16[384,512]{1,0:T(8,128)(2,1)S(1)} %fusion.6, f32[512]{0:T(512)S(1)} %bitcast.59, pred[384]{0:T(512)(128)(4,1)S(1)} %iota_compare_fusion.5, s32[384,384]{1,0:T(8,128)S(1)} %copy-done.2), kind=kOutput, calls=%fused_computation.14 | convolution fusion | flops 152125440 | bytes 2951552 | tf_op jit(solution)/shard_map/dot_general | solution.py:18
  98.0 0.0 copy-done.9
  (9 shorter events, 0.1 us)
Async XLA Ops:
  0.6 51.3 %copy-start = (bf16[512,512]{1,0:T(8,128)(2,1)S(1)}, bf16[512,512]{1,0:T(8,128)(2,1)}, u32[]{:S(2)}) copy-start(bf16[512,512]{1,0:T(8,128)(2,1)} %param.14) | copy-start | bytes 1572868
  2.7 10.5 %copy-start.10 = (s32[1,32,8]{1,2,0:T(8,128)S(1)}, s32[1,32,8]{1,2,0:T(8,128)}, u32[]{:S(2)}) copy-start(s32[1,32,8]{1,2,0:T(8,128)} %param.21) | copy-start | bytes 3076
  2.7 18.2 %all-to-all-start = ((bf16[8,4,128]{2,1,0:T(4,128)(2,1)}), bf16[8,4,128]{2,1,0:T(4,128)(2,1)S(1)}, u32[]{:S(2)}, u32[]{:S(2)}) async-start(bf16[8,4,128]{2,1,0:T(4,128)(2,1)} %broadcast_in_dim.51), calls=%async_computation | async-start | bytes 16384 | tf_op jit(solution)/shard_map/all_to_all | solution.py:26
  13.3 0.7 copy-start.12
  21.8 11.0 %copy-start.7 = (s32[384,512]{1,0:T(8,128)S(1)}, s32[384,512]{1,0:T(8,128)}, u32[]{:S(2)}) copy-start(s32[384,512]{1,0:T(8,128)} %param.18) | copy-start | bytes 2359300
  21.8 26.5 %all-to-all-start.1 = ((bf16[32,16,512]{2,1,0:T(8,128)(2,1)}), bf16[32,16,512]{2,1,0:T(8,128)(2,1)S(1)}, u32[]{:S(2)}, u32[]{:S(2)}) async-start(bf16[32,16,512]{2,1,0:T(8,128)(2,1)} %pad_maximum_fusion), calls=%async_computation.1 | async-start | bytes 1048576 | tf_op jit(solution)/shard_map/all_to_all | solution.py:26
  32.1 0.7 copy-start.11
  32.8 1.2 %copy-start.1 = (bf16[384,512]{1,0:T(8,128)(2,1)S(1)}, bf16[384,512]{1,0:T(8,128)(2,1)}, u32[]{:S(2)}) copy-start(bf16[384,512]{1,0:T(8,128)(2,1)} %param.12) | copy-start | bytes 1179652
  32.8 1.2 %copy-start.4 = (bf16[512,512]{1,0:T(8,128)(2,1)S(1)}, bf16[512,512]{1,0:T(8,128)(2,1)}, u32[]{:S(2)}) copy-start(bf16[512,512]{1,0:T(8,128)(2,1)} %param.13) | copy-start | bytes 1572868
  34.0 1.3 %copy-start.2 = (s32[384,384]{1,0:T(8,128)S(1)}, s32[384,384]{1,0:T(8,128)}, u32[]{:S(2)}) copy-start(s32[384,384]{1,0:T(8,128)} %param.17) | copy-start | bytes 1769476
  48.3 2.5 %copy-start.5 = (s32[384,256]{1,0:T(8,128)S(1)}, s32[384,256]{1,0:T(8,128)}, u32[]{:S(2)}) copy-start(s32[384,256]{1,0:T(8,128)} %param.20) | copy-start | bytes 1179652
  50.8 1.2 %copy-start.6 = (f32[384,512]{1,0:T(8,128)S(1)}, f32[384,512]{1,0:T(8,128)}, u32[]{:S(2)}) copy-start(f32[384,512]{1,0:T(8,128)} %convolution_add_fusion) | copy-start | bytes 2359300
  50.8 1.2 %copy-start.13 = (f32[512]{0:T(512)S(1)}, f32[512]{0:T(512)}, u32[]{:S(2)}) copy-start(f32[512]{0:T(512)} %param.15) | copy-start | bytes 6148
  55.5 1.7 %copy-start.8 = (bf16[512,384]{1,0:T(8,128)(2,1)S(1)}, bf16[512,384]{1,0:T(8,128)(2,1)}, u32[]{:S(2)}) copy-start(bf16[512,384]{1,0:T(8,128)(2,1)} %convolution_convert_fusion) | copy-start | bytes 1179652
  57.5 3.4 %collective-permute-start = (bf16[256,512]{1,0:T(8,128)(2,1)S(1)}, bf16[256,512]{1,0:T(8,128)(2,1)S(1)}, u32[]{:S(2)}, u32[]{:S(2)}) collective-permute-start(bf16[256,512]{1,0:T(8,128)(2,1)S(1)} %convolution_convert_fusion.1), channel_id=1, source_target_pairs={{0,32},{32,0},{1,33},{33,1},{2,34},{34,2},{3,35},{35,3},{4,36},{36... | collective-permute-start | bytes 786440 | tf_op jit(solution)/shard_map/ppermute | solution.py:85
  62.2 22.8 %all-to-all-start.2 = ((bf16[32,16,512]{2,1,0:T(8,128)(2,1)}), bf16[32,16,512]{2,1,0:T(8,128)(2,1)S(1)}, u32[]{:S(2)}, u32[]{:S(2)}) async-start(bf16[32,16,512]{2,1,0:T(8,128)(2,1)} %pad_maximum_fusion.1), calls=%async_computation.2 | async-start | bytes 1048576 | tf_op jit(solution)/shard_map/all_to_all | solution.py:26
  84.9 0.8 copy-start.3
  85.7 11.0 %all-to-all-start.3 = ((f32[8,4,128]{2,1,0:T(4,128)}), f32[8,4,128]{2,1,0:T(4,128)S(1)}, u32[]{:S(2)}, u32[]{:S(2)}) async-start(f32[8,4,128]{2,1,0:T(4,128)} %reshape.175), calls=%async_computation.3 | async-start | bytes 32768 | tf_op jit(solution)/shard_map/all_to_all | solution.py:26
  96.8 1.2 %copy-start.9 = (f32[4,128]{1,0:T(4,128)}, f32[4,128]{1,0:T(4,128)S(1)}, u32[]{:S(2)}) copy-start(f32[4,128]{1,0:T(4,128)S(1)} %reduce_sum.19) | copy-start | bytes 6148

commit v2 on v1

v2 whole, which is shorter than its diff:
```python
import jax
import jax.numpy as jnp
from jax import lax
from jax.experimental import pallas as pl
from jax.experimental.pallas import tpu as pltpu
from jax.sharding import Mesh
from jax.sharding import PartitionSpec as P

ALL = ("z", "core", "x", "y")
DOM = ("x", "y")
F32 = jnp.float32
BF16 = jnp.bfloat16
LANES = 128
ROWS = 16
CORES, PEERS = 2, 32


def matmul(lhs, rhs):
    return jnp.dot(lhs, rhs, preferred_element_type=F32)


def transposed(matrix, other):
    return lax.dot_general(matrix, other, (((0,), (0,)), ((), ())), preferred_element_type=F32)


def back_product(grads, weight):
    return lax.dot_general(grads, weight, (((1,), (1,)), ((), ())), preferred_element_type=F32)


def exchange(parts, axis):
    return lax.all_to_all(parts, axis, split_axis=0, concat_axis=0, tiled=True)


def split_lanes(rows):
    parts = [rows[:, k : k + LANES] for k in range(0, rows.shape[1], LANES)]
    return jnp.stack(parts, axis=1)


def in_vmem(body, name, shapes, operands, flops, limit=8, untouched=0):
    spec = pl.BlockSpec(memory_space=pltpu.VMEM)
    moved = sum(x.size * x.dtype.itemsize for x in (*operands, *shapes)) if flops else 0
    return pl.pallas_call(
        body,
        out_shape=shapes,
        in_specs=[spec] * (len(operands) - untouched) + [pl.BlockSpec(memory_space=pl.ANY)] * untouched,
        out_specs=[spec] * len(shapes),
        compiler_params=pltpu.CompilerParams(vmem_limit_bytes=limit * 1024 * 1024),
        cost_estimate=pl.CostEstimate(flops=flops, bytes_accessed=moved, transcendentals=0),
        name=name,
    )(*operands)


def hub_row_kernel(place_ref, rows_ref, out_ref, block, sem):
    row = place_ref[0, 0]
    first = pl.multiple_of(row // ROWS * ROWS, ROWS)
    copy = pltpu.make_async_copy(rows_ref.at[pl.ds(first, ROWS)], block, sem)
    copy.start()
    copy.wait()
    at = lax.broadcasted_iota(jnp.int32, block.shape, 0) == row - first
    own = jnp.sum(jnp.where(at, block[...].astype(F32), 0.0), axis=0, keepdims=True)
    out_ref[...] = jnp.broadcast_to(split_lanes(own), out_ref.shape)


def hub_row(hub_rows, features, n_z):
    width = features.shape[1]
    return pl.pallas_call(
        hub_row_kernel,
        out_shape=jax.ShapeDtypeStruct((n_z, width // LANES, LANES), F32),
        in_specs=[pl.BlockSpec(memory_space=pltpu.SMEM), pl.BlockSpec(memory_space=pl.ANY)],
        out_specs=pl.BlockSpec(memory_space=pltpu.VMEM),
        scratch_shapes=[pltpu.VMEM((ROWS, width), BF16), pltpu.SemaphoreType.DMA],
        compiler_params=pltpu.CompilerParams(vmem_limit_bytes=60 * 1024 * 1024),
        name="hub_row",
    )(hub_rows, features)


def payload_kernel(along_z, outgoing, out_ref):
    peers, rows, width = out_ref.shape
    hubs = jnp.concatenate([along_z[:, k, :] for k in range(width // LANES)], axis=1)
    hubs = jnp.broadcast_to(hubs[None], (peers, *hubs.shape))
    slots = outgoing[...].astype(F32).reshape(peers, -1, width)
    out_ref[...] = jnp.concatenate([slots, hubs], axis=1).astype(BF16)


def adjacency_kernel(hub_adj, remote_adj, hub_mat, hub_t, remote_mat, remote_t):
    hubs, slots = hub_t.shape[0], remote_t.shape[0]
    n_z = hubs // (CORES * PEERS)

    def source(place):
        at_core, at_peer, at_z = place // (PEERS * n_z), (place // n_z) % PEERS, place % n_z
        return (at_z * CORES + at_core) * PEERS + at_peer

    first = lax.broadcasted_iota(jnp.int32, (hubs, hubs), 0)
    second = lax.broadcasted_iota(jnp.int32, (hubs, hubs), 1)
    hub_rows = hub_adj[...].astype(BF16)
    hub_mat[...] = matmul(hub_rows, (source(second) == first).astype(BF16)).astype(BF16)
    hub_t[...] = back_product((source(first) == second).astype(BF16), hub_rows).astype(BF16)
    remote_rows = remote_adj[...].astype(BF16)
    remote_mat[...] = remote_rows
    same = (first == second)[:slots, :slots].astype(BF16)
    remote_t[...] = back_product(same, remote_rows).astype(BF16)


def middle_kernel(
    hubs, hub_mat, incoming, remote_mat, base, inverse, weight, base_pre, grad, out_ref, pre_ref, mean_ref
):
    peers, width = incoming.shape[0], incoming.shape[2]
    received = incoming[...].astype(F32)[:, : remote_mat.shape[1] // peers]
    received = received.reshape(remote_mat.shape[1], width).astype(BF16)
    total = matmul(hub_mat[...], hubs[...]) + matmul(remote_mat[...], received)
    scale = jnp.concatenate([inverse[...]] * (total.shape[1] // LANES), axis=1)
    mean_feats = ((total + base[...]) * scale).astype(BF16)
    preact = matmul(mean_feats, weight[...]) + base_pre[...]
    low = jnp.minimum(preact, 0.0)
    grown = jnp.exp(low)
    near = low * (1.0 + low * (0.5 + low * (1.0 / 6.0)))
    below = jnp.where(low > -0.02, near, grown - 1.0)
    out_ref[...] = jnp.where(preact > 0, preact, below).astype(BF16)
    grad_pre = (grad[...].astype(F32) * grown).astype(BF16)
    pre_ref[...] = grad_pre
    mean_ref[...] = (back_product(grad_pre, weight[...]) * scale).astype(BF16)


def pack_kernel(remote_t, grad_mean, hub_t, both_means, out_ref):
    peers, rows, width = out_ref.shape
    slots = matmul(remote_t[...], grad_mean[...]).reshape(peers, -1, width)
    nodes = grad_mean.shape[0]
    hubs = matmul(hub_t[0], both_means[:nodes]) + matmul(hub_t[1], both_means[nodes:])
    hubs = hubs.reshape(peers, -1, width)
    out_ref[...] = jnp.concatenate([slots, hubs], axis=1).astype(BF16)


def arrive_kernel(returned, base, out_ref):
    del base
    total = jnp.sum(returned[...].astype(F32), axis=0)
    out_ref[...] = split_lanes(total[total.shape[0] - out_ref.shape[0] :])


def tail_kernel(pick, returned, base, out_ref):
    out_ref[...] = base[...] + matmul(pick[...], returned[...])


def on_device(
    features,
    w_self,
    w_neigh,
    bias_term,
    degree,
    local_adj,
    hub_adj,
    hub_rows,
    remote_adj,
    send_rows,
    send_counts,
    grad_out,
):
    nodes, width = features.shape
    n_z, n_core = lax.axis_size("z"), lax.axis_size("core")
    peers, slots = send_rows.shape[1:]
    hubs = hub_adj.shape[1]
    half = hubs // n_core
    block = slots + n_z
    first_core = lax.axis_index("core") == 0
    rows_f32 = jax.ShapeDtypeStruct((nodes, width), F32)
    rows_b16 = jax.ShapeDtypeStruct((nodes, width), BF16)

    along_z = exchange(hub_row(hub_rows, features, n_z), "z")

    live = jnp.arange(slots, dtype=jnp.int32)[None, :] < send_counts[0][:, None]
    picked = jnp.where(live, send_rows[0], -1)
    at_node = jnp.arange(nodes, dtype=jnp.int32)[:, None]
    pick = (picked.reshape(1, peers * slots) == at_node).astype(BF16)
    outgoing = transposed(pick, features).astype(BF16)
    (payload,) = in_vmem(
        payload_kernel,
        "payload",
        [jax.ShapeDtypeStruct((peers, block, width), BF16)],
        (along_z, outgoing),
        flops=peers * block * width,
    )
    incoming = exchange(payload, DOM)
    same_core = incoming[:, slots:].reshape(half, width)
    all_hubs = lax.all_gather(same_core, "core", axis=0, tiled=True)

    hub_mat, hub_t, remote_mat, remote_t = in_vmem(
        adjacency_kernel,
        "adjacency",
        [jax.ShapeDtypeStruct(shape, BF16) for shape in ((nodes, hubs), (hubs, nodes), (nodes, peers * slots), (peers * slots, nodes))],
        (hub_adj, remote_adj),
        flops=0,
        limit=56,
    )
    chip_t = lax.all_gather(hub_t, "core", axis=0).reshape(n_core, n_core, half, nodes)
    chip_t = jnp.where(first_core, chip_t[:, 0], chip_t[:, 1])
    local_mat = local_adj.astype(BF16)

    base = features.astype(F32) + matmul(local_mat, features)
    base_pre = matmul(features, w_self) + bias_term
    inverse = jnp.broadcast_to(1.0 / (degree.astype(F32)[:, None] + 1.0), (nodes, LANES))
    out_feats, grad_pre, grad_mean = in_vmem(
        middle_kernel,
        "middle",
        [rows_b16] * 3,
        (all_hubs, hub_mat, incoming, remote_mat, base, inverse, w_neigh, base_pre, grad_out),
        flops=2 * nodes * width * (hubs + peers * slots + 2 * width),
    )

    both_means = lax.all_gather(grad_mean, "core", axis=0, tiled=True)
    (payload,) = in_vmem(
        pack_kernel,
        "pack",
        [jax.ShapeDtypeStruct((peers, block, width), BF16)],
        (remote_t, grad_mean, chip_t, both_means),
        flops=2 * 3 * half * nodes * width,
    )
    returned = exchange(payload, DOM)
    grad_base = back_product(grad_pre, w_self) + grad_mean.astype(F32) + transposed(local_mat, grad_mean)
    shape = jax.ShapeDtypeStruct((n_z, width // LANES, LANES), F32)
    (hub_z,) = in_vmem(arrive_kernel, "arrive", [shape], (returned, grad_base), flops=half * width, untouched=1)
    hub_parts = exchange(hub_z, "z")
    hub_grad = jnp.sum(hub_parts, axis=0).reshape(1, width)

    wide = jnp.concatenate([picked, jnp.full((peers, n_z), -1, jnp.int32)], axis=1)
    wide_pick = (wide.reshape(1, peers * block) == at_node).astype(BF16)
    (grad_local,) = in_vmem(
        tail_kernel,
        "tail",
        [rows_f32],
        (wide_pick, returned.reshape(peers * block, width), grad_base),
        flops=2 * nodes * peers * block * width,
    )
    at_hub = at_node == hub_rows[0, 0]
    grad_features = (grad_local + jnp.where(at_hub, hub_grad, 0.0)).astype(BF16)
    return (out_feats, grad_features, hub_grad)


def solution(mesh):
    fine = Mesh(mesh.devices.reshape(8, 2, 4, 8), ALL)
    rows, whole = P(ALL), P()
    return jax.shard_map(
        on_device,
        mesh=fine,
        in_specs=(rows, whole, whole, whole, rows, rows, rows, rows, rows, rows, rows, rows),
        out_specs=(rows, rows, rows),
        check_vma=False,
    )
```

time: 98.7 us -> 95 us (0.963)
  matrix products: 16.5 us -> 1.89 us
  Pallas kernels: 0 us -> 9.2 us
  blocking collectives: 2.45 us -> 7.17 us
  waiting for transfers between devices: 40.8 us -> 36.8 us
  local copies, waits for them, and re-layouts: 3.75 us -> 5.33 us
    pallas_call x0 -> x7, Pallas kernels: none -> 9.2 us  [the longest x6 7.85 us: in_vmem(): pl.pallas_call(body, out_shape=shapes, in_specs=[spec] * (len(operands) -...]
    dot_general x6 -> x2, matrix products: 9.74 us -> 0.73 us  [matmul(): return jnp.dot(lhs, rhs, preferred_element_type=F32)]
    all_gather x0 -> x2, blocking collectives: none -> 4.86 us  [the longest x1 2.49 us: on_device(): both_means = lax.all_gather(grad_mean, 'core', axis=0, tiled=True)]
    unnamed x30 -> x38, local copies, waits for them, and re-layouts: 1.49 us -> 4.84 us
    all_to_all x4, waiting for transfers between devices: 39.8 us -> 36.8 us  [exchange(): return lax.all_to_all(parts, axis, split_axis=0, concat_axis=0, tiled=True)]
    dot_general x2 -> x1, matrix products: 3.33 us -> 0.4 us  [back_product(): lax.dot_general(grads, weight, (((1,), (1,)), ((), ())), preferred_elemen...]
    dot_general x5 -> x2, matrix products: 3.44 us -> 0.76 us  [transposed(): lax.dot_general(matrix, other, (((0,), (0,)), ((), ())), preferred_elemen...]
    ppermute x1 -> x0, starting transfers between devices: 2.04 us -> none  [on_device(): lax.ppermute(transposed(other, grad_mean).astype(BF16), 'core', [(0, 1),...]
  transfers between devices with their start and end apart: 5 -> 4, of which waited for: 5 -> 4; matrix products, arithmetic and copies ran while one was open for 9% -> 4% of each run, Pallas kernels for 0% -> 3%
where the time goes in v2:
time: 95 us; the launch traced here: 94.3 us
  waiting for transfers between devices  36.8 us (39%)
  starting transfers between devices  30.4 us (32%)
  Pallas kernels  9.2 us (10%)
  blocking collectives  7.17 us (8%)
  local copies, waits for them, and re-layouts  5.33 us (6%)
  matrix products  1.89 us (2%)
  other arithmetic  1.84 us (2%)
  between operations  1.58 us (2%)
    all_to_all x4, waiting for transfers between devices, exchange(): return lax.all_to_all(parts, axis, split_axis=0, concat_axis=0, tiled=True)  36.8 us
    all_to_all x4, starting transfers between devices, exchange(): return lax.all_to_all(parts, axis, split_axis=0, concat_axis=0, tiled=True)  30.4 us
    pallas_call x6, Pallas kernels, in_vmem(): pl.pallas_call(body, out_shape=shapes, in_specs=[spec] * (len(operands) -...  7.85 us
    unnamed x38, local copies, waits for them, and re-layouts  4.84 us
    all_gather x1, blocking collectives, on_device(): both_means = lax.all_gather(grad_mean, 'core', axis=0, tiled=True)  2.49 us
    all_gather x1, blocking collectives, on_device(): lax.all_gather(hub_t, 'core', axis=0).reshape(n_core, n_core, half, nodes)  2.37 us
    all_gather x1, blocking collectives, on_device(): all_hubs = lax.all_gather(same_core, 'core', axis=0, tiled=True)  2.31 us
  transfers between devices with their start and end apart: 4, of which 4 were waited for; matrix products, arithmetic and copies ran while one was open for 4% of the time, Pallas kernels for 3%

profile of v2, /device:TPU:8, one launch (start us, length us, event | category | flops | bytes accessed | tf_op | source)
XLA Modules:
  0.0 94.3 jit_solution(7596658248044210354)
XLA Ops:
  0.6 0.0 copy-start
  0.6 0.0 copy-start.9
  1.4 1.3 %hub_row.1 = f32[8,4,128]{2,1,0:T(4,128)} custom-call(s32[1,1]{1,0:T(1,128)} %copy.26.place_ref, bf16[384,512]{1,0:T(8,128)(2,1)} %rows_ref.1), custom_call_target="tpu_custom_call" | custom-call | tf_op jit(solution)/shard_map/hub_row/pallas_call | solution.py:66
  2.7 10.3 %all-to-all-start = ((f32[8,4,128]{2,1,0:T(4,128)}), f32[8,4,128]{2,1,0:T(4,128)S(1)}, u32[]{:S(2)}, u32[]{:S(2)}) async-start(f32[8,4,128]{2,1,0:T(4,128)} %hub_row.1), calls=%async_computation | async-start | bytes 32768 | tf_op jit(solution)/shard_map/all_to_all | solution.py:31
  13.1 0.0 copy-start.17
  13.1 0.7 copy-done.17
  13.7 0.0 copy-start.13
  13.7 0.1 copy.16
  13.8 0.1 lt.26
  13.9 0.5 copy-done.13
  14.4 0.1 copy.17
  14.5 0.1 squeeze.10
  14.6 0.0 copy-done.9
  14.6 0.3 convolution_convert_fusion.outgoing
  15.0 2.8 %adjacency.1 = (bf16[384,512]{1,0:T(8,128)(2,1)}, bf16[512,384]{1,0:T(8,128)(2,1)}, bf16[384,256]{1,0:T(8,128)(2,1)}, bf16[256,384]{1,0:T(8,128)(2,1)}) custom-call(s32[384,512]{1,0:T(8,128)} %hub_adj.1, s32[384,256]{1,0:T(8,128)} %remote_adj.1), custom_call_target="tpu_custom_call" | custom-call | tf_op jit(solution)/shard_map/adjacency/pallas_call | solution.py:42
  17.7 3.1 %all-to-all-done.along_z = f32[8,4,128]{2,1,0:T(4,128)S(1)} async-done(((f32[8,4,128]{2,1,0:T(4,128)}), f32[8,4,128]{2,1,0:T(4,128)S(1)}, u32[]{:S(2)}, u32[]{:S(2)}) %all-to-all-start) | async-done | bytes 16416 | tf_op jit(solution)/shard_map/all_to_all | solution.py:31
  20.8 0.9 payload.1
  21.7 0.0 copy-start.12
  21.7 10.3 %all-to-all-start.1 = ((bf16[32,16,512]{2,1,0:T(8,128)(2,1)}), bf16[32,16,512]{2,1,0:T(8,128)(2,1)S(1)}, u32[]{:S(2)}, u32[]{:S(2)}) async-start(bf16[32,16,512]{2,1,0:T(8,128)(2,1)} %payload.1), calls=%async_computation.1 | async-start | bytes 1048576 | tf_op jit(solution)/shard_map/all_to_all | solution.py:31
  32.0 0.0 copy-done.12
  32.0 2.4 %all-gather = bf16[1024,384]{1,0:T(8,128)(2,1)S(1)} all-gather(bf16[512,384]{1,0:T(8,128)(2,1)S(1)} %copy-done.12), channel_id=2, replica_groups=mesh['z'=8,'core'=2,'x'=4,'y'=8] {'core'}, dimensions={0}, use_global_device_ids=true | all-gather | bytes 1179648 | tf_op jit(solution)/shard_map/all_gather | solution.py:193
  34.4 0.0 copy-start.16
  34.4 0.7 copy-done.16
  35.1 0.0 copy-start.15
  35.1 0.8 fusion.3.hub_t
  35.9 0.0 copy-done
  35.9 0.0 copy-done.15
  35.9 0.0 copy-start.10
  35.9 0.4 convolution_add_fusion.2.base_pre
  36.3 0.7 copy-done.10
  37.0 0.4 convolution_add_fusion.base
  37.3 10.9 %all-to-all-done.1.incoming = bf16[32,16,512]{2,1,0:T(8,128)(2,1)S(1)} async-done(((bf16[32,16,512]{2,1,0:T(8,128)(2,1)}), bf16[32,16,512]{2,1,0:T(8,128)(2,1)S(1)}, u32[]{:S(2)}, u32[]{:S(2)}) %all-to-all-start.1) | async-done | bytes 524320 | tf_op jit(solution)/shard_map/all_to_all | solution.py:31
  48.2 0.0 copy-start.4
  48.2 0.0 copy-start.7
  48.2 0.0 copy-start.2
  48.2 0.0 copy-start.3
  48.3 2.3 %all_gather.12.hubs = bf16[512,512]{1,0:T(8,128)(2,1)S(1)} all-gather(bf16[256,512]{1,0:T(8,128)(2,1)S(1)} %slice_bitcast_fusion.2), channel_id=1, replica_groups=mesh['z'=8,'core'=2,'x'=4,'y'=8] {'core'}, dimensions={0}, use_global_device_ids=true | all-gather | bytes 786432 | tf_op jit(solution)/shard_map/all_gather | solution.py:183
  50.6 0.1 broadcast_in_dim.39.inverse
  50.7 0.0 copy-done.4
  50.7 0.0 copy-done.7
  50.7 0.0 copy-done.2
  50.7 0.0 copy-done.3
  50.7 1.8 %middle.1 = (bf16[384,512]{1,0:T(8,128)(2,1)}, bf16[384,512]{1,0:T(8,128)(2,1)S(1)}, bf16[384,512]{1,0:T(8,128)(2,1)S(1)}) custom-call(bf16[512,512]{1,0:T(8,128)(2,1)S(1)} %all_gather.12.hubs, bf16[384,512]{1,0:T(8,128)(2,1)S(1)} %copy-done.4, bf16[32,16,512]{2,1,0:T(8,128)(2,1)S(1)} %all-to-all-done.1.incoming, bf16[384,256]{1,0:T(8,128)(2,1)S(1)} %copy-done.7, ...), custom_call_target="tpu_custom_call" | custom-call | flops 704643072 | bytes 5505024 | tf_op jit(solution)/shard_map/middle/pallas_call | solution.py:42
  52.5 0.7 copy-done.5
  53.3 2.5 %all_gather.15.both_means = bf16[768,512]{1,0:T(8,128)(2,1)S(1)} all-gather(bf16[384,512]{1,0:T(8,128)(2,1)S(1)} %get-tuple-element.14.grad_mean), channel_id=1, replica_groups=mesh['z'=8,'core'=2,'x'=4,'y'=8] {'core'}, dimensions={0}, use_global_device_ids=true | all-gather | bytes 1179648 | tf_op jit(solution)/shard_map/all_gather | solution.py:208
  55.8 0.0 copy-done.1
  55.8 0.0 copy-done.8
  55.8 1.4 %pack.1 = bf16[32,16,512]{2,1,0:T(8,128)(2,1)} custom-call(bf16[256,384]{1,0:T(8,128)(2,1)S(1)} %copy-done.8, bf16[384,512]{1,0:T(8,128)(2,1)S(1)} %get-tuple-element.14.grad_mean, bf16[2,256,384]{2,1,0:T(8,128)(2,1)S(1)} %copy-done.1, bf16[768,512]{1,0:T(8,128)(2,1)S(1)} %all_gather.15.both_means), custom_call_target="tpu_custom_call" | custom-call | flops 301989888 | bytes 2293760 | tf_op jit(solution)/shard_map/pack/pallas_call | solution.py:42
  57.2 4.8 %all-to-all-start.2 = ((bf16[32,16,512]{2,1,0:T(8,128)(2,1)}), bf16[32,16,512]{2,1,0:T(8,128)(2,1)S(1)}, u32[]{:S(2)}, u32[]{:S(2)}) async-start(bf16[32,16,512]{2,1,0:T(8,128)(2,1)} %pack.1), calls=%async_computation.2 | async-start | bytes 1048576 | tf_op jit(solution)/shard_map/all_to_all | solution.py:31
  62.0 0.0 copy-start.6
  62.0 0.1 copy.25
  62.1 0.1 eq.45
  62.2 0.1 fusion.1.pick
  62.3 0.7 copy-done.6
  63.0 0.4 convolution_add_fusion.1
  63.4 0.7 copy-done.11
  64.1 0.4 fusion.base
  64.5 15.4 %all-to-all-done.2.returned = bf16[32,16,512]{2,1,0:T(8,128)(2,1)S(1)} async-done(((bf16[32,16,512]{2,1,0:T(8,128)(2,1)}), bf16[32,16,512]{2,1,0:T(8,128)(2,1)S(1)}, u32[]{:S(2)}, u32[]{:S(2)}) %all-to-all-start.2) | async-done | bytes 524320 | tf_op jit(solution)/shard_map/all_to_all | solution.py:31
  79.9 0.7 arrive.1
  80.6 5.0 %all-to-all-start.3 = ((f32[8,4,128]{2,1,0:T(4,128)}), f32[8,4,128]{2,1,0:T(4,128)S(1)}, u32[]{:S(2)}, u32[]{:S(2)}) async-start(f32[8,4,128]{2,1,0:T(4,128)} %arrive.1), calls=%async_computation.3 | async-start | bytes 32768 | tf_op jit(solution)/shard_map/all_to_all | solution.py:31
  85.6 0.4 tail.1
  86.0 7.4 %all-to-all-done.3 = f32[8,4,128]{2,1,0:T(4,128)S(1)} async-done(((f32[8,4,128]{2,1,0:T(4,128)}), f32[8,4,128]{2,1,0:T(4,128)S(1)}, u32[]{:S(2)}, u32[]{:S(2)}) %all-to-all-start.3) | async-done | bytes 16416 | tf_op jit(solution)/shard_map/all_to_all | solution.py:31
  93.4 0.9 add_convert_fusion
  94.3 0.0 copy-done.14
  (13 shorter events, 0.1 us)
Async XLA Ops:
  0.6 35.3 %copy-start = (bf16[512,512]{1,0:T(8,128)(2,1)S(1)}, bf16[512,512]{1,0:T(8,128)(2,1)}, u32[]{:S(2)}) copy-start(bf16[512,512]{1,0:T(8,128)(2,1)} %param.13) | copy-start | bytes 1572868
  0.6 13.9 %copy-start.9 = (bf16[384,512]{1,0:T(8,128)(2,1)S(1)}, bf16[384,512]{1,0:T(8,128)(2,1)}, u32[]{:S(2)}) copy-start(bf16[384,512]{1,0:T(8,128)(2,1)} %rows_ref.1) | copy-start | bytes 1179652
  2.7 18.1 %all-to-all-start = ((f32[8,4,128]{2,1,0:T(4,128)}), f32[8,4,128]{2,1,0:T(4,128)S(1)}, u32[]{:S(2)}, u32[]{:S(2)}) async-start(f32[8,4,128]{2,1,0:T(4,128)} %hub_row.1), calls=%async_computation | async-start | bytes 32768 | tf_op jit(solution)/shard_map/all_to_all | solution.py:31
  13.1 0.7 copy-start.17
  13.7 0.7 copy-start.13
  21.7 10.3 %copy-start.12 = (bf16[512,384]{1,0:T(8,128)(2,1)S(1)}, bf16[512,384]{1,0:T(8,128)(2,1)}, u32[]{:S(2)}) copy-start(bf16[512,384]{1,0:T(8,128)(2,1)} %get-tuple-element.15) | copy-start | bytes 1179652
  21.7 26.5 %all-to-all-start.1 = ((bf16[32,16,512]{2,1,0:T(8,128)(2,1)}), bf16[32,16,512]{2,1,0:T(8,128)(2,1)S(1)}, u32[]{:S(2)}, u32[]{:S(2)}) async-start(bf16[32,16,512]{2,1,0:T(8,128)(2,1)} %payload.1), calls=%async_computation.1 | async-start | bytes 1048576 | tf_op jit(solution)/shard_map/all_to_all | solution.py:31
  34.4 0.7 copy-start.16
  35.1 0.8 copy-start.15
  35.9 1.1 %copy-start.10 = (s32[384,384]{1,0:T(8,128)S(1)}, s32[384,384]{1,0:T(8,128)}, u32[]{:S(2)}) copy-start(s32[384,384]{1,0:T(8,128)} %param.17) | copy-start | bytes 1769476
  48.2 2.5 %copy-start.4 = (bf16[384,512]{1,0:T(8,128)(2,1)S(1)}, bf16[384,512]{1,0:T(8,128)(2,1)}, u32[]{:S(2)}) copy-start(bf16[384,512]{1,0:T(8,128)(2,1)} %get-tuple-element.10.hub_mat) | copy-start | bytes 1179652
  48.2 2.5 %copy-start.7 = (bf16[384,256]{1,0:T(8,128)(2,1)S(1)}, bf16[384,256]{1,0:T(8,128)(2,1)}, u32[]{:S(2)}) copy-start(bf16[384,256]{1,0:T(8,128)(2,1)} %get-tuple-element.11.remote_mat) | copy-start | bytes 589828
  48.2 2.5 %copy-start.2 = (bf16[512,512]{1,0:T(8,128)(2,1)S(1)}, bf16[512,512]{1,0:T(8,128)(2,1)}, u32[]{:S(2)}) copy-start(bf16[512,512]{1,0:T(8,128)(2,1)} %weight.1) | copy-start | bytes 1572868
  48.2 2.5 %copy-start.3 = (bf16[384,512]{1,0:T(8,128)(2,1)S(1)}, bf16[384,512]{1,0:T(8,128)(2,1)}, u32[]{:S(2)}) copy-start(bf16[384,512]{1,0:T(8,128)(2,1)} %grad.1) | copy-start | bytes 1179652
  52.5 0.7 copy-start.5
  53.3 2.5 %copy-start.1 = (bf16[2,256,384]{2,1,0:T(8,128)(2,1)S(1)}, bf16[2,256,384]{2,1,0:T(8,128)(2,1)}, u32[]{:S(2)}) copy-start(bf16[2,256,384]{2,1,0:T(8,128)(2,1)} %fusion.3.hub_t) | copy-start | bytes 1179652
  53.3 2.5 %copy-start.8 = (bf16[256,384]{1,0:T(8,128)(2,1)S(1)}, bf16[256,384]{1,0:T(8,128)(2,1)}, u32[]{:S(2)}) copy-start(bf16[256,384]{1,0:T(8,128)(2,1)} %get-tuple-element.13.remote_t) | copy-start | bytes 589828
  57.2 22.8 %all-to-all-start.2 = ((bf16[32,16,512]{2,1,0:T(8,128)(2,1)}), bf16[32,16,512]{2,1,0:T(8,128)(2,1)S(1)}, u32[]{:S(2)}, u32[]{:S(2)}) async-start(bf16[32,16,512]{2,1,0:T(8,128)(2,1)} %pack.1), calls=%async_computation.2 | async-start | bytes 1048576 | tf_op jit(solution)/shard_map/all_to_all | solution.py:31
  62.0 1.0 %copy-start.6 = (bf16[384,512]{1,0:T(8,128)(2,1)S(1)}, bf16[384,512]{1,0:T(8,128)(2,1)}, u32[]{:S(2)}) copy-start(bf16[384,512]{1,0:T(8,128)(2,1)} %copy-done.5) | copy-start | bytes 1179652
  63.0 1.1 %copy-start.11 = (s32[384,384]{1,0:T(8,128)S(1)}, s32[384,384]{1,0:T(8,128)}, u32[]{:S(2)}) copy-start(s32[384,384]{1,0:T(8,128)} %param.17) | copy-start | bytes 1769476
  80.6 12.8 %all-to-all-start.3 = ((f32[8,4,128]{2,1,0:T(4,128)}), f32[8,4,128]{2,1,0:T(4,128)S(1)}, u32[]{:S(2)}, u32[]{:S(2)}) async-start(f32[8,4,128]{2,1,0:T(4,128)} %arrive.1), calls=%async_computation.3 | async-start | bytes 32768 | tf_op jit(solution)/shard_map/all_to_all | solution.py:31
  93.4 0.9 copy-start.14

commit v3 on v2

--- a/solution.py
+++ b/solution.py
@@ -6,8 +6,7 @@
 from jax.sharding import Mesh
 from jax.sharding import PartitionSpec as P
 
-ALL = ("z", "core", "x", "y")
-DOM = ("x", "y")
+ALL = ("z", "core", "dom")
 F32 = jnp.float32
 BF16 = jnp.bfloat16
 LANES = 128
@@ -15,6 +14,20 @@
 CORES, PEERS = 2, 32
 
 
+def peer_at(place):
+    place = (place + 18) % PEERS
+    return place % 4 * 8 + place // 4
+
+
+PEER_ORDER = [peer_at(k) for k in range(PEERS)]
+PEER_PLACE = [PEER_ORDER.index(k) for k in range(PEERS)]
+Z_ORDER = [4, 5, 6, 7, 0, 1, 2, 3]
+
+
+def taken(blocks, places):
+    return jnp.concatenate([blocks[k : k + 1] for k in places], axis=0)
+
+
 def matmul(lhs, rhs):
     return jnp.dot(lhs, rhs, preferred_element_type=F32)
 
@@ -27,8 +40,9 @@
     return lax.dot_general(grads, weight, (((1,), (1,)), ((), ())), preferred_element_type=F32)
 
 
-def exchange(parts, axis):
-    return lax.all_to_all(parts, axis, split_axis=0, concat_axis=0, tiled=True)
+def exchange(parts, axis, order=None):
+    groups = None if order is None else [order]
+    return lax.all_to_all(parts, axis, split_axis=0, concat_axis=0, tiled=True, axis_index_groups=groups)
 
 
 def split_lanes(rows):
@@ -36,18 +50,32 @@
     return jnp.stack(parts, axis=1)
 
 
-def in_vmem(body, name, shapes, operands, flops, limit=8, untouched=0):
-    spec = pl.BlockSpec(memory_space=pltpu.VMEM)
+def in_vmem(body, name, shapes, operands, flops, limit=8, untouched=0, sent=()):
+    spec, anywhere = pl.BlockSpec(memory_space=pltpu.VMEM), pl.BlockSpec(memory_space=pltpu.HBM)
     moved = sum(x.size * x.dtype.itemsize for x in (*operands, *shapes)) if flops else 0
+    scratch = [pltpu.VMEM(shapes[k].shape, shapes[k].dtype) for k in sent]
     return pl.pallas_call(
         body,
         out_shape=shapes,
         in_specs=[spec] * (len(operands) - untouched) + [pl.BlockSpec(memory_space=pl.ANY)] * untouched,
-        out_specs=[spec] * len(shapes),
+        out_specs=[anywhere if k in sent else spec for k in range(len(shapes))],
+        scratch_shapes=scratch + [pltpu.SemaphoreType.DMA((2,))] if sent else [],
         compiler_params=pltpu.CompilerParams(vmem_limit_bytes=limit * 1024 * 1024),
         cost_estimate=pl.CostEstimate(flops=flops, bytes_accessed=moved, transcendentals=0),
         name=name,
     )(*operands)
+
+
+def in_halves(out_ref, held, sem, value):
+    half = out_ref.shape[-1] // 2
+    copies = []
+    for k in range(2):
+        columns = slice(k * half, (k + 1) * half)
+        held[..., columns] = value(columns)
+        copies.append(pltpu.make_async_copy(held.at[..., columns], out_ref.at[..., columns], sem.at[k]))
+        copies[k].start()
+    for copy in copies:
+        copy.wait()
 
 
 def hub_row_kernel(place_ref, rows_ref, out_ref, block, sem):
@@ -74,12 +102,17 @@
     )(hub_rows, features)
 
 
-def payload_kernel(along_z, outgoing, out_ref):
-    peers, rows, width = out_ref.shape
-    hubs = jnp.concatenate([along_z[:, k, :] for k in range(width // LANES)], axis=1)
-    hubs = jnp.broadcast_to(hubs[None], (peers, *hubs.shape))
-    slots = outgoing[...].astype(F32).reshape(peers, -1, width)
-    out_ref[...] = jnp.concatenate([slots, hubs], axis=1).astype(BF16)
+def payload_kernel(along_z, outgoing, out_ref, held, sem):
+    peers = out_ref.shape[0]
+
+    def value(columns):
+        parts = [along_z[:, k // LANES, :] for k in range(columns.start, columns.stop, LANES)]
+        hubs = jnp.concatenate(parts, axis=1)
+        hubs = jnp.broadcast_to(hubs[None], (peers, *hubs.shape))
+        slots = outgoing[:, columns].astype(F32).reshape(peers, -1, hubs.shape[2])
+        return jnp.concatenate([taken(slots, PEER_ORDER), hubs], axis=1).astype(BF16)
+
+    in_halves(out_ref, held, sem, value)
 
 
 def adjacency_kernel(hub_adj, remote_adj, hub_mat, hub_t, remote_mat, remote_t):
@@ -88,7 +121,7 @@
 
     def source(place):
         at_core, at_peer, at_z = place // (PEERS * n_z), (place // n_z) % PEERS, place % n_z
-        return (at_z * CORES + at_core) * PEERS + at_peer
+        return (at_z * CORES + at_core) * PEERS + peer_at(at_peer)
 
     first = lax.broadcasted_iota(jnp.int32, (hubs, hubs), 0)
     second = lax.broadcasted_iota(jnp.int32, (hubs, hubs), 1)
@@ -102,11 +135,11 @@
 
 
 def middle_kernel(
-    hubs, hub_mat, incoming, remote_mat, base, inverse, weight, base_pre, grad, out_ref, pre_ref, mean_ref
+    hubs, hub_mat, incoming, remote_mat, base, inverse, weight, base_pre, grad, out_ref, pre_ref, mean_ref, out, pre, sem
 ):
     peers, width = incoming.shape[0], incoming.shape[2]
     received = incoming[...].astype(F32)[:, : remote_mat.shape[1] // peers]
-    received = received.reshape(remote_mat.shape[1], width).astype(BF16)
+    received = taken(received, PEER_PLACE).reshape(remote_mat.shape[1], width).astype(BF16)
     total = matmul(hub_mat[...], hubs[...]) + matmul(remote_mat[...], received)
     scale = jnp.concatenate([inverse[...]] * (total.shape[1] // LANES), axis=1)
     mean_feats = ((total + base[...]) * scale).astype(BF16)
@@ -115,29 +148,53 @@
     grown = jnp.exp(low)
     near = low * (1.0 + low * (0.5 + low * (1.0 / 6.0)))
     below = jnp.where(low > -0.02, near, grown - 1.0)
-    out_ref[...] = jnp.where(preact > 0, preact, below).astype(BF16)
+    out[...] = jnp.where(preact > 0, preact, below).astype(BF16)
     grad_pre = (grad[...].astype(F32) * grown).astype(BF16)
-    pre_ref[...] = grad_pre
+    pre[...] = grad_pre
+    copies = [pltpu.make_async_copy(*pair, sem.at[k]) for k, pair in enumerate(((out, out_ref), (pre, pre_ref)))]
+    for copy in copies:
+        copy.start()
     mean_ref[...] = (back_product(grad_pre, weight[...]) * scale).astype(BF16)
-
-
-def pack_kernel(remote_t, grad_mean, hub_t, both_means, out_ref):
-    peers, rows, width = out_ref.shape
-    slots = matmul(remote_t[...], grad_mean[...]).reshape(peers, -1, width)
-    nodes = grad_mean.shape[0]
-    hubs = matmul(hub_t[0], both_means[:nodes]) + matmul(hub_t[1], both_means[nodes:])
-    hubs = hubs.reshape(peers, -1, width)
-    out_ref[...] = jnp.concatenate([slots, hubs], axis=1).astype(BF16)
+    for copy in copies:
+        copy.wait()
+
+
+def pack_kernel(remote_t, grad_mean, hub_t, both_means, grad_pre, out_ref, held, sem):
+    del grad_pre
+    peers, nodes = out_ref.shape[0], grad_mean.shape[0]
+
+    def value(columns):
+        slots = matmul(remote_t[...], grad_mean[:, columns])
+        hubs = matmul(hub_t[0], both_means[:nodes, columns]) + matmul(hub_t[1], both_means[nodes:, columns])
+        slots, hubs = (x.reshape(peers, -1, x.shape[1]) for x in (slots, hubs))
+        return jnp.concatenate([taken(slots, PEER_ORDER), hubs], axis=1).astype(BF16)
+
+    in_halves(out_ref, held, sem, value)
 
 
 def arrive_kernel(returned, base, out_ref):
     del base
     total = jnp.sum(returned[...].astype(F32), axis=0)
-    out_ref[...] = split_lanes(total[total.shape[0] - out_ref.shape[0] :])
-
-
-def tail_kernel(pick, returned, base, out_ref):
-    out_ref[...] = base[...] + matmul(pick[...], returned[...])
+    out_ref[...] = taken(split_lanes(total[total.shape[0] - out_ref.shape[0] :]), Z_ORDER)
+
+
+def tail_kernel(pick, returned, base, at_hub, out_ref):
+    del at_hub
+    blocks = taken(returned[...], PEER_PLACE)
+    out_ref[...] = base[...] + matmul(pick[...], blocks.reshape(-1, blocks.shape[2]))
+
+
+def last_kernel(grad_local, at_hub, parts, out_ref, hub_ref, held, held_hub, sem):
+    total = jnp.sum(parts[...], axis=0)
+    hub = jnp.concatenate([total[k : k + 1] for k in range(total.shape[0])], axis=1)
+    held_hub[...] = hub
+    here = jnp.concatenate([at_hub[...]] * total.shape[0], axis=1) > 0
+    held[...] = (grad_local[...] + jnp.where(here, hub, 0.0)).astype(BF16)
+    copies = [pltpu.make_async_copy(*pair, sem.at[k]) for k, pair in enumerate(((held, out_ref), (held_hub, hub_ref)))]
+    for copy in copies:
+        copy.start()
+    for copy in copies:
+        copy.wait()
 
 
 def on_device(
@@ -177,8 +234,9 @@
         [jax.ShapeDtypeStruct((peers, block, width), BF16)],
         (along_z, outgoing),
         flops=peers * block * width,
-    )
-    incoming = exchange(payload, DOM)
+        sent=(0,),
+    )
+    incoming = exchange(payload, "dom", PEER_ORDER)
     same_core = incoming[:, slots:].reshape(half, width)
     all_hubs = lax.all_gather(same_core, "core", axis=0, tiled=True)
 
@@ -203,6 +261,7 @@
         [rows_b16] * 3,
         (all_hubs, hub_mat, incoming, remote_mat, base, inverse, w_neigh, base_pre, grad_out),
         flops=2 * nodes * width * (hubs + peers * slots + 2 * width),
+        sent=(0, 1),
     )
 
     both_means = lax.all_gather(grad_mean, "core", axis=0, tiled=True)
@@ -210,15 +269,17 @@
         pack_kernel,
         "pack",
         [jax.ShapeDtypeStruct((peers, block, width), BF16)],
-        (remote_t, grad_mean, chip_t, both_means),
+        (remote_t, grad_mean, chip_t, both_means, grad_pre),
         flops=2 * 3 * half * nodes * width,
-    )
-    returned = exchange(payload, DOM)
+        untouched=1,
+        sent=(0,),
+    )
+    returned = exchange(payload, "dom", PEER_ORDER)
     grad_base = back_product(grad_pre, w_self) + grad_mean.astype(F32) + transposed(local_mat, grad_mean)
     shape = jax.ShapeDtypeStruct((n_z, width // LANES, LANES), F32)
+    at_hub = jnp.broadcast_to((at_node == hub_rows[0, 0]).astype(F32), (nodes, LANES))
     (hub_z,) = in_vmem(arrive_kernel, "arrive", [shape], (returned, grad_base), flops=half * width, untouched=1)
-    hub_parts = exchange(hub_z, "z")
-    hub_grad = jnp.sum(hub_parts, axis=0).reshape(1, width)
+    hub_parts = exchange(hub_z, "z", Z_ORDER)
 
     wide = jnp.concatenate([picked, jnp.full((peers, n_z), -1, jnp.int32)], axis=1)
     wide_pick = (wide.reshape(1, peers * block) == at_node).astype(BF16)
@@ -226,16 +287,23 @@
         tail_kernel,
         "tail",
         [rows_f32],
-        (wide_pick, returned.reshape(peers * block, width), grad_base),
+        (wide_pick, returned, grad_base, at_hub),
         flops=2 * nodes * peers * block * width,
-    )
-    at_hub = at_node == hub_rows[0, 0]
-    grad_features = (grad_local + jnp.where(at_hub, hub_grad, 0.0)).astype(BF16)
+        untouched=1,
+    )
+    grad_features, hub_grad = in_vmem(
+        last_kernel,
+        "last",
+        [rows_b16, jax.ShapeDtypeStruct((1, width), F32)],
+        (grad_local, at_hub, hub_parts),
+        flops=nodes * width,
+        sent=(0, 1),
+    )
     return (out_feats, grad_features, hub_grad)
 
 
 def solution(mesh):
-    fine = Mesh(mesh.devices.reshape(8, 2, 4, 8), ALL)
+    fine = Mesh(mesh.devices.reshape(8, CORES, PEERS), ALL)
     rows, whole = P(ALL), P()
     return jax.shard_map(
         on_device,

time: 95 us -> 87.2 us (0.918)
  waiting for transfers between devices: 36.8 us -> 22.2 us
  starting transfers between devices: 30.4 us -> 37.7 us
  Pallas kernels: 9.2 us -> 10.3 us
    all_to_all x4, waiting for transfers between devices: 36.8 us -> 22.2 us  [exchange(): lax.all_to_all(parts, axis, split_axis=0, concat_axis=0, tiled=True, axis...]
    all_to_all x4, starting transfers between devices: 30.4 us -> 37.7 us  [exchange(): lax.all_to_all(parts, axis, split_axis=0, concat_axis=0, tiled=True, axis...]
    pallas_call x6 -> x7, Pallas kernels: 7.85 us -> 8.97 us  [in_vmem(): pl.pallas_call(body, out_shape=shapes, in_specs=[spec] * (len(operands) -...]
    unnamed x38 -> x36, local copies, waits for them, and re-layouts: 4.84 us -> 4.1 us
  transfers between devices with their start and end apart: 4 -> 4, of which waited for: 4 -> 4; matrix products, arithmetic and copies ran while one was open for 4% -> 4% of each run, Pallas kernels for 3% -> 4%
where the time goes in v3:
time: 87.2 us; the launch traced here: 86.5 us
  starting transfers between devices  37.7 us (43%)
  waiting for transfers between devices  22.2 us (25%)
  Pallas kernels  10.3 us (12%)
  blocking collectives  7.18 us (8%)
  local copies, waits for them, and re-layouts  4.7 us (5%)
  matrix products  1.89 us (2%)
  between operations  1.63 us (2%)
  other arithmetic  0.93 us (1%)
    all_to_all x4, starting transfers between devices, exchange(): lax.all_to_all(parts, axis, split_axis=0, concat_axis=0, tiled=True, axis...  37.7 us
    all_to_all x4, waiting for transfers between devices, exchange(): lax.all_to_all(parts, axis, split_axis=0, concat_axis=0, tiled=True, axis...  22.2 us
    pallas_call x7, Pallas kernels, in_vmem(): pl.pallas_call(body, out_shape=shapes, in_specs=[spec] * (len(operands) -...  8.97 us
    unnamed x36, local copies, waits for them, and re-layouts  4.1 us
    all_gather x1, blocking collectives, on_device(): both_means = lax.all_gather(grad_mean, 'core', axis=0, tiled=True)  2.5 us
    all_gather x1, blocking collectives, on_device(): lax.all_gather(hub_t, 'core', axis=0).reshape(n_core, n_core, half, nodes)  2.37 us
    all_gather x1, blocking collectives, on_device(): all_hubs = lax.all_gather(same_core, 'core', axis=0, tiled=True)  2.31 us
  transfers between devices with their start and end apart: 4, of which 4 were waited for; matrix products, arithmetic and copies ran while one was open for 4% of the time, Pallas kernels for 4%

profile of v3, /device:TPU:8, one launch (start us, length us, event | category | flops | bytes accessed | tf_op | source)
XLA Modules:
  0.0 86.5 jit_solution(509625881885860531)
XLA Ops:
  0.6 0.0 copy-start
  0.6 0.0 copy-start.9
  1.4 1.3 %hub_row.1 = f32[8,4,128]{2,1,0:T(4,128)} custom-call(s32[1,1]{1,0:T(1,128)} %copy.26.place_ref, bf16[384,512]{1,0:T(8,128)(2,1)} %rows_ref.1), custom_call_target="tpu_custom_call" | custom-call | tf_op jit(solution)/shard_map/hub_row/pallas_call | solution.py:94
  2.7 10.3 %all-to-all-start = ((f32[8,4,128]{2,1,0:T(4,128)}), f32[8,4,128]{2,1,0:T(4,128)S(1)}, u32[]{:S(2)}, u32[]{:S(2)}) async-start(f32[8,4,128]{2,1,0:T(4,128)} %hub_row.1), calls=%async_computation | async-start | bytes 32768 | tf_op jit(solution)/shard_map/all_to_all | solution.py:45
  13.1 0.0 copy-start.16
  13.1 0.7 copy-done.16
  13.7 0.0 copy-start.13
  13.7 0.1 copy.16
  13.8 0.1 lt.26
  13.9 0.5 copy-done.13
  14.4 0.1 copy.17
  14.5 0.1 squeeze.10
  14.6 0.0 copy-done.9
  14.6 0.3 convolution_convert_fusion.outgoing
  15.0 3.0 %adjacency.1 = (bf16[384,512]{1,0:T(8,128)(2,1)}, bf16[512,384]{1,0:T(8,128)(2,1)}, bf16[384,256]{1,0:T(8,128)(2,1)}, bf16[256,384]{1,0:T(8,128)(2,1)}) custom-call(s32[384,512]{1,0:T(8,128)} %hub_adj.1, s32[384,256]{1,0:T(8,128)} %remote_adj.1), custom_call_target="tpu_custom_call" | custom-call | tf_op jit(solution)/shard_map/adjacency/pallas_call | solution.py:57
  18.0 2.8 %all-to-all-done.along_z = f32[8,4,128]{2,1,0:T(4,128)S(1)} async-done(((f32[8,4,128]{2,1,0:T(4,128)}), f32[8,4,128]{2,1,0:T(4,128)S(1)}, u32[]{:S(2)}, u32[]{:S(2)}) %all-to-all-start) | async-done | bytes 16416 | tf_op jit(solution)/shard_map/all_to_all | solution.py:45
  20.8 0.9 payload.1
  21.7 0.0 copy-start.12
  21.7 11.1 %all-to-all-start.1 = ((bf16[32,16,512]{2,1,0:T(8,128)(2,1)}), bf16[32,16,512]{2,1,0:T(8,128)(2,1)S(1)}, u32[]{:S(2)}, u32[]{:S(2)}) async-start(bf16[32,16,512]{2,1,0:T(8,128)(2,1)} %payload.1), calls=%async_computation.1 | async-start | bytes 1048576 | tf_op jit(solution)/shard_map/all_to_all | solution.py:45
  32.8 0.0 copy-done.12
  32.8 2.4 %all-gather = bf16[1024,384]{1,0:T(8,128)(2,1)S(1)} all-gather(bf16[512,384]{1,0:T(8,128)(2,1)S(1)} %copy-done.12), channel_id=2, replica_groups=mesh['z'=8,'core'=2,'dom'=32] {'core'}, dimensions={0}, use_global_device_ids=true | all-gather | bytes 1179648 | tf_op jit(solution)/shard_map/all_gather | solution.py:251
  35.2 0.0 copy-start.15
  35.2 0.7 copy-done.15
  35.9 0.0 copy-start.14
  35.9 0.8 fusion.3.hub_t
  36.7 0.0 copy-done
  36.7 0.0 copy-done.14
  36.7 0.4 convolution_add_fusion.2.base_pre
  37.1 0.7 copy-done.10
  37.8 0.4 convolution_add_fusion.base
  38.1 6.4 %all-to-all-done.1.incoming = bf16[32,16,512]{2,1,0:T(8,128)(2,1)S(1)} async-done(((bf16[32,16,512]{2,1,0:T(8,128)(2,1)}), bf16[32,16,512]{2,1,0:T(8,128)(2,1)S(1)}, u32[]{:S(2)}, u32[]{:S(2)}) %all-to-all-start.1) | async-done | bytes 524320 | tf_op jit(solution)/shard_map/all_to_all | solution.py:45
  44.5 0.0 copy-start.4
  44.6 0.0 copy-start.5
  44.6 2.3 %all_gather.12.hubs = bf16[512,512]{1,0:T(8,128)(2,1)S(1)} all-gather(bf16[256,512]{1,0:T(8,128)(2,1)S(1)} %slice_bitcast_fusion.2), channel_id=1, replica_groups=mesh['z'=8,'core'=2,'dom'=32] {'core'}, dimensions={0}, use_global_device_ids=true | all-gather | bytes 786432 | tf_op jit(solution)/shard_map/all_gather | solution.py:241
  46.9 0.1 broadcast_in_dim.11.inverse
  47.0 0.0 copy-done.6
  47.0 0.0 copy-done.7
  47.0 0.0 copy-done.4
  47.0 0.0 copy-done.5
  47.0 1.9 %middle.1 = (bf16[384,512]{1,0:T(8,128)(2,1)}, bf16[384,512]{1,0:T(8,128)(2,1)S(1)}, bf16[384,512]{1,0:T(8,128)(2,1)S(1)}) custom-call(bf16[512,512]{1,0:T(8,128)(2,1)S(1)} %all_gather.12.hubs, bf16[384,512]{1,0:T(8,128)(2,1)S(1)} %copy-done.6, bf16[32,16,512]{2,1,0:T(8,128)(2,1)S(1)} %all-to-all-done.1.incoming, bf16[384,256]{1,0:T(8,128)(2,1)S(1)} %copy-done.7, ...), custom_call_target="tpu_custom_call" | custom-call | flops 704643072 | bytes 5505024 | tf_op jit(solution)/shard_map/middle/pallas_call | solution.py:57
  48.9 0.0 copy-start.1
  48.9 0.0 copy-start.3
  48.9 0.0 copy-start.8
  48.9 2.5 %all_gather.15.both_means = bf16[768,512]{1,0:T(8,128)(2,1)S(1)} all-gather(bf16[384,512]{1,0:T(8,128)(2,1)S(1)} %get-tuple-element.16.grad_mean), channel_id=1, replica_groups=mesh['z'=8,'core'=2,'dom'=32] {'core'}, dimensions={0}, use_global_device_ids=true | all-gather | bytes 1179648 | tf_op jit(solution)/shard_map/all_gather | solution.py:267
  51.4 0.0 copy-done.1
  51.4 0.0 copy-done.3
  51.4 0.0 copy-done.8
  51.4 1.3 %pack.1 = bf16[32,16,512]{2,1,0:T(8,128)(2,1)} custom-call(bf16[256,384]{1,0:T(8,128)(2,1)S(1)} %copy-done.8, bf16[384,512]{1,0:T(8,128)(2,1)S(1)} %get-tuple-element.16.grad_mean, bf16[2,256,384]{2,1,0:T(8,128)(2,1)S(1)} %copy-done.3, bf16[768,512]{1,0:T(8,128)(2,1)S(1)} %all_gather.15.both_means, bf16[384,512]{1,0:T(8,128)(2,1)S(1)} %get-tuple-element.18.grad_pre), custom_call_target="tpu_custom_call" | custom-call | flops 301989888 | bytes 2686976 | tf_op jit(solution)/shard_map/pack/pallas_call | solution.py:57
  52.8 9.1 %all-to-all-start.2 = ((bf16[32,16,512]{2,1,0:T(8,128)(2,1)}), bf16[32,16,512]{2,1,0:T(8,128)(2,1)S(1)}, u32[]{:S(2)}, u32[]{:S(2)}) async-start(bf16[32,16,512]{2,1,0:T(8,128)(2,1)} %pack.1), calls=%async_computation.2 | async-start | bytes 1048576 | tf_op jit(solution)/shard_map/all_to_all | solution.py:45
  61.9 0.0 copy-start.2
  61.9 0.1 copy.25
  62.0 0.1 eq.45
  62.1 0.1 fusion.1.pick
  62.2 0.7 copy-done.2
  62.9 0.4 convolution_add_fusion.1
  63.3 0.7 copy-done.11
  64.0 0.4 fusion.base
  64.4 11.0 %all-to-all-done.2.returned = bf16[32,16,512]{2,1,0:T(8,128)(2,1)S(1)} async-done(((bf16[32,16,512]{2,1,0:T(8,128)(2,1)}), bf16[32,16,512]{2,1,0:T(8,128)(2,1)S(1)}, u32[]{:S(2)}, u32[]{:S(2)}) %all-to-all-start.2) | async-done | bytes 524320 | tf_op jit(solution)/shard_map/all_to_all | solution.py:45
  75.4 0.7 arrive.1
  76.0 7.2 %all-to-all-start.3 = ((f32[8,4,128]{2,1,0:T(4,128)}), f32[8,4,128]{2,1,0:T(4,128)S(1)}, u32[]{:S(2)}, u32[]{:S(2)}) async-start(f32[8,4,128]{2,1,0:T(4,128)} %arrive.1), calls=%async_computation.3 | async-start | bytes 32768 | tf_op jit(solution)/shard_map/all_to_all | solution.py:45
  83.2 0.1 broadcast_in_dim.24.at_hub
  83.3 0.4 tail.1.grad_local
  83.7 2.0 %all-to-all-done.3.parts = f32[8,4,128]{2,1,0:T(4,128)S(1)} async-done(((f32[8,4,128]{2,1,0:T(4,128)}), f32[8,4,128]{2,1,0:T(4,128)S(1)}, u32[]{:S(2)}, u32[]{:S(2)}) %all-to-all-start.3) | async-done | bytes 16416 | tf_op jit(solution)/shard_map/all_to_all | solution.py:45
  85.7 0.8 last.1
  (11 shorter events, 0.1 us)
Async XLA Ops:
  0.6 36.1 %copy-start = (bf16[512,512]{1,0:T(8,128)(2,1)S(1)}, bf16[512,512]{1,0:T(8,128)(2,1)}, u32[]{:S(2)}) copy-start(bf16[512,512]{1,0:T(8,128)(2,1)} %param.13) | copy-start | bytes 1572868
  0.6 13.9 %copy-start.9 = (bf16[384,512]{1,0:T(8,128)(2,1)S(1)}, bf16[384,512]{1,0:T(8,128)(2,1)}, u32[]{:S(2)}) copy-start(bf16[384,512]{1,0:T(8,128)(2,1)} %rows_ref.1) | copy-start | bytes 1179652
  2.7 18.1 %all-to-all-start = ((f32[8,4,128]{2,1,0:T(4,128)}), f32[8,4,128]{2,1,0:T(4,128)S(1)}, u32[]{:S(2)}, u32[]{:S(2)}) async-start(f32[8,4,128]{2,1,0:T(4,128)} %hub_row.1), calls=%async_computation | async-start | bytes 32768 | tf_op jit(solution)/shard_map/all_to_all | solution.py:45
  13.1 0.7 copy-start.16
  13.7 0.7 copy-start.13
  21.7 11.1 %copy-start.12 = (bf16[512,384]{1,0:T(8,128)(2,1)S(1)}, bf16[512,384]{1,0:T(8,128)(2,1)}, u32[]{:S(2)}) copy-start(bf16[512,384]{1,0:T(8,128)(2,1)} %get-tuple-element.17) | copy-start | bytes 1179652
  21.7 22.8 %all-to-all-start.1 = ((bf16[32,16,512]{2,1,0:T(8,128)(2,1)}), bf16[32,16,512]{2,1,0:T(8,128)(2,1)S(1)}, u32[]{:S(2)}, u32[]{:S(2)}) async-start(bf16[32,16,512]{2,1,0:T(8,128)(2,1)} %payload.1), calls=%async_computation.1 | async-start | bytes 1048576 | tf_op jit(solution)/shard_map/all_to_all | solution.py:45
  35.2 0.7 copy-start.15
  35.9 0.8 copy-start.14
  36.7 1.1 %copy-start.10 = (s32[384,384]{1,0:T(8,128)S(1)}, s32[384,384]{1,0:T(8,128)}, u32[]{:S(2)}) copy-start(s32[384,384]{1,0:T(8,128)} %param.17) | copy-start | bytes 1769476
  44.5 2.5 %copy-start.6 = (bf16[384,512]{1,0:T(8,128)(2,1)S(1)}, bf16[384,512]{1,0:T(8,128)(2,1)}, u32[]{:S(2)}) copy-start(bf16[384,512]{1,0:T(8,128)(2,1)} %get-tuple-element.12.hub_mat) | copy-start | bytes 1179652
  44.5 2.5 %copy-start.7 = (bf16[384,256]{1,0:T(8,128)(2,1)S(1)}, bf16[384,256]{1,0:T(8,128)(2,1)}, u32[]{:S(2)}) copy-start(bf16[384,256]{1,0:T(8,128)(2,1)} %get-tuple-element.13.remote_mat) | copy-start | bytes 589828
  44.5 2.5 %copy-start.4 = (bf16[512,512]{1,0:T(8,128)(2,1)S(1)}, bf16[512,512]{1,0:T(8,128)(2,1)}, u32[]{:S(2)}) copy-start(bf16[512,512]{1,0:T(8,128)(2,1)} %weight.1) | copy-start | bytes 1572868
  44.6 2.5 %copy-start.5 = (bf16[384,512]{1,0:T(8,128)(2,1)S(1)}, bf16[384,512]{1,0:T(8,128)(2,1)}, u32[]{:S(2)}) copy-start(bf16[384,512]{1,0:T(8,128)(2,1)} %grad.1) | copy-start | bytes 1179652
  48.9 2.5 %copy-start.1 = (bf16[384,512]{1,0:T(8,128)(2,1)}, bf16[384,512]{1,0:T(8,128)(2,1)S(1)}, u32[]{:S(2)}) copy-start(bf16[384,512]{1,0:T(8,128)(2,1)S(1)} %get-tuple-element.18.grad_pre) | copy-start | bytes 1179652
  48.9 2.5 %copy-start.3 = (bf16[2,256,384]{2,1,0:T(8,128)(2,1)S(1)}, bf16[2,256,384]{2,1,0:T(8,128)(2,1)}, u32[]{:S(2)}) copy-start(bf16[2,256,384]{2,1,0:T(8,128)(2,1)} %fusion.3.hub_t) | copy-start | bytes 1179652
  48.9 2.5 %copy-start.8 = (bf16[256,384]{1,0:T(8,128)(2,1)S(1)}, bf16[256,384]{1,0:T(8,128)(2,1)}, u32[]{:S(2)}) copy-start(bf16[256,384]{1,0:T(8,128)(2,1)} %get-tuple-element.15.remote_t) | copy-start | bytes 589828
  52.8 22.6 %all-to-all-start.2 = ((bf16[32,16,512]{2,1,0:T(8,128)(2,1)}), bf16[32,16,512]{2,1,0:T(8,128)(2,1)S(1)}, u32[]{:S(2)}, u32[]{:S(2)}) async-start(bf16[32,16,512]{2,1,0:T(8,128)(2,1)} %pack.1), calls=%async_computation.2 | async-start | bytes 1048576 | tf_op jit(solution)/shard_map/all_to_all | solution.py:45
  61.9 1.0 %copy-start.2 = (bf16[384,512]{1,0:T(8,128)(2,1)S(1)}, bf16[384,512]{1,0:T(8,128)(2,1)}, u32[]{:S(2)}) copy-start(bf16[384,512]{1,0:T(8,128)(2,1)} %copy-done.1) | copy-start | bytes 1179652
  62.9 1.1 %copy-start.11 = (s32[384,384]{1,0:T(8,128)S(1)}, s32[384,384]{1,0:T(8,128)}, u32[]{:S(2)}) copy-start(s32[384,384]{1,0:T(8,128)} %param.17) | copy-start | bytes 1769476
  76.0 9.7 %all-to-all-start.3 = ((f32[8,4,128]{2,1,0:T(4,128)}), f32[8,4,128]{2,1,0:T(4,128)S(1)}, u32[]{:S(2)}, u32[]{:S(2)}) async-start(f32[8,4,128]{2,1,0:T(4,128)} %arrive.1), calls=%async_computation.3 | async-start | bytes 32768 | tf_op jit(solution)/shard_map/all_to_all | solution.py:45

commit v4 on v3

--- a/solution.py
+++ b/solution.py
@@ -15,8 +15,8 @@
 
 
 def peer_at(place):
-    place = (place + 18) % PEERS
-    return place % 4 * 8 + place // 4
+    place = (place + 18) & (PEERS - 1)
+    return ((place & 3) << 3) | (place >> 2)
 
 
 PEER_ORDER = [peer_at(k) for k in range(PEERS)]
@@ -118,19 +118,20 @@
 def adjacency_kernel(hub_adj, remote_adj, hub_mat, hub_t, remote_mat, remote_t):
     hubs, slots = hub_t.shape[0], remote_t.shape[0]
     n_z = hubs // (CORES * PEERS)
+    shift = n_z.bit_length() - 1
 
     def source(place):
-        at_core, at_peer, at_z = place // (PEERS * n_z), (place // n_z) % PEERS, place % n_z
+        at_core, at_peer, at_z = place >> shift + 5, (place >> shift) & (PEERS - 1), (place + Z_ORDER[0]) & (n_z - 1)
         return (at_z * CORES + at_core) * PEERS + peer_at(at_peer)
 
-    first = lax.broadcasted_iota(jnp.int32, (hubs, hubs), 0)
-    second = lax.broadcasted_iota(jnp.int32, (hubs, hubs), 1)
+    column = lax.broadcasted_iota(jnp.int32, (hubs, 1), 0)
+    row = lax.broadcasted_iota(jnp.int32, (1, hubs), 1)
     hub_rows = hub_adj[...].astype(BF16)
-    hub_mat[...] = matmul(hub_rows, (source(second) == first).astype(BF16)).astype(BF16)
-    hub_t[...] = back_product((source(first) == second).astype(BF16), hub_rows).astype(BF16)
+    hub_mat[...] = matmul(hub_rows, (source(row) == column).astype(BF16)).astype(BF16)
+    hub_t[...] = back_product((source(column) == row).astype(BF16), hub_rows).astype(BF16)
     remote_rows = remote_adj[...].astype(BF16)
     remote_mat[...] = remote_rows
-    same = (first == second)[:slots, :slots].astype(BF16)
+    same = (column[:slots] == row[:, :slots]).astype(BF16)
     remote_t[...] = back_product(same, remote_rows).astype(BF16)
 
 
@@ -175,7 +176,7 @@
 def arrive_kernel(returned, base, out_ref):
     del base
     total = jnp.sum(returned[...].astype(F32), axis=0)
-    out_ref[...] = taken(split_lanes(total[total.shape[0] - out_ref.shape[0] :]), Z_ORDER)
+    out_ref[...] = split_lanes(total[total.shape[0] - out_ref.shape[0] :])
 
 
 def tail_kernel(pick, returned, base, at_hub, out_ref):
@@ -221,7 +222,7 @@
     rows_f32 = jax.ShapeDtypeStruct((nodes, width), F32)
     rows_b16 = jax.ShapeDtypeStruct((nodes, width), BF16)
 
-    along_z = exchange(hub_row(hub_rows, features, n_z), "z")
+    along_z = exchange(hub_row(hub_rows, features, n_z), "z", Z_ORDER)
 
     live = jnp.arange(slots, dtype=jnp.int32)[None, :] < send_counts[0][:, None]
     picked = jnp.where(live, send_rows[0], -1)

time: 87.2 us -> 88.2 us (1.011)
  starting transfers between devices: 37.7 us -> 40.8 us
  waiting for transfers between devices: 22.2 us -> 20.2 us
    all_to_all x4, starting transfers between devices: 37.7 us -> 40.8 us  [exchange(): lax.all_to_all(parts, axis, split_axis=0, concat_axis=0, tiled=True, axis...]
    all_to_all x4, waiting for transfers between devices: 22.2 us -> 20.2 us  [exchange(): lax.all_to_all(parts, axis, split_axis=0, concat_axis=0, tiled=True, axis...]
  transfers between devices with their start and end apart: 4 -> 4, of which waited for: 4 -> 3; matrix products, arithmetic and copies ran while one was open for 4% -> 4% of each run, Pallas kernels for 4% -> 4%
where the time goes in v4:
time: 88.2 us; the launch traced here: 87.4 us
  starting transfers between devices  40.8 us (46%)
  waiting for transfers between devices  20.2 us (23%)
  Pallas kernels  10.1 us (11%)
  blocking collectives  7.18 us (8%)
  local copies, waits for them, and re-layouts  4.7 us (5%)
  matrix products  1.89 us (2%)
  between operations  1.63 us (2%)
  other arithmetic  0.93 us (1%)
    all_to_all x4, starting transfers between devices, exchange(): lax.all_to_all(parts, axis, split_axis=0, concat_axis=0, tiled=True, axis...  40.8 us
    all_to_all x4, waiting for transfers between devices, exchange(): lax.all_to_all(parts, axis, split_axis=0, concat_axis=0, tiled=True, axis...  20.2 us
    pallas_call x7, Pallas kernels, in_vmem(): pl.pallas_call(body, out_shape=shapes, in_specs=[spec] * (len(operands) -...  8.75 us
    unnamed x36, local copies, waits for them, and re-layouts  4.11 us
    all_gather x1, blocking collectives, on_device(): both_means = lax.all_gather(grad_mean, 'core', axis=0, tiled=True)  2.5 us
    all_gather x1, blocking collectives, on_device(): lax.all_gather(hub_t, 'core', axis=0).reshape(n_core, n_core, half, nodes)  2.37 us
    all_gather x1, blocking collectives, on_device(): all_hubs = lax.all_gather(same_core, 'core', axis=0, tiled=True)  2.31 us
  transfers between devices with their start and end apart: 4, of which 3 were waited for; matrix products, arithmetic and copies ran while one was open for 4% of the time, Pallas kernels for 4%

profile of v4, /device:TPU:8, one launch (start us, length us, event | category | flops | bytes accessed | tf_op | source)
XLA Modules:
  0.0 87.4 jit_solution(146794795923748560)
XLA Ops:
  0.6 0.0 copy-start
  0.6 0.0 copy-start.9
  1.4 1.3 %hub_row.1 = f32[8,4,128]{2,1,0:T(4,128)} custom-call(s32[1,1]{1,0:T(1,128)} %copy.26.place_ref, bf16[384,512]{1,0:T(8,128)(2,1)} %rows_ref.1), custom_call_target="tpu_custom_call" | custom-call | tf_op jit(solution)/shard_map/hub_row/pallas_call | solution.py:94
  2.7 13.6 %all-to-all-start = ((f32[8,4,128]{2,1,0:T(4,128)}), f32[8,4,128]{2,1,0:T(4,128)S(1)}, u32[]{:S(2)}, u32[]{:S(2)}) async-start(f32[8,4,128]{2,1,0:T(4,128)} %hub_row.1), calls=%async_computation | async-start | bytes 32768 | tf_op jit(solution)/shard_map/all_to_all | solution.py:45
  16.3 0.0 copy-start.16
  16.3 0.7 copy-done.16
  17.0 0.0 copy-start.13
  17.0 0.1 copy.16
  17.1 0.1 lt.26
  17.2 0.5 copy-done.13
  17.7 0.1 copy.17
  17.7 0.1 squeeze.10
  17.9 0.0 copy-done.9
  17.9 0.4 convolution_convert_fusion.outgoing
  18.2 2.8 %adjacency.1 = (bf16[384,512]{1,0:T(8,128)(2,1)}, bf16[512,384]{1,0:T(8,128)(2,1)}, bf16[384,256]{1,0:T(8,128)(2,1)}, bf16[256,384]{1,0:T(8,128)(2,1)}) custom-call(s32[384,512]{1,0:T(8,128)} %hub_adj.1, s32[384,256]{1,0:T(8,128)} %remote_adj.1), custom_call_target="tpu_custom_call" | custom-call | tf_op jit(solution)/shard_map/adjacency/pallas_call | solution.py:57
  21.0 0.0 all-to-all-done.along_z
  21.1 0.9 payload.1
  21.9 0.0 copy-start.12
  21.9 11.1 %all-to-all-start.1 = ((bf16[32,16,512]{2,1,0:T(8,128)(2,1)}), bf16[32,16,512]{2,1,0:T(8,128)(2,1)S(1)}, u32[]{:S(2)}, u32[]{:S(2)}) async-start(bf16[32,16,512]{2,1,0:T(8,128)(2,1)} %payload.1), calls=%async_computation.1 | async-start | bytes 1048576 | tf_op jit(solution)/shard_map/all_to_all | solution.py:45
  33.0 0.0 copy-done.12
  33.0 2.4 %all-gather = bf16[1024,384]{1,0:T(8,128)(2,1)S(1)} all-gather(bf16[512,384]{1,0:T(8,128)(2,1)S(1)} %copy-done.12), channel_id=2, replica_groups=mesh['z'=8,'core'=2,'dom'=32] {'core'}, dimensions={0}, use_global_device_ids=true | all-gather | bytes 1179648 | tf_op jit(solution)/shard_map/all_gather | solution.py:252
  35.4 0.0 copy-start.15
  35.4 0.7 copy-done.15
  36.1 0.0 copy-start.14
  36.1 0.8 fusion.3.hub_t
  36.9 0.0 copy-done
  36.9 0.0 copy-done.14
  36.9 0.4 convolution_add_fusion.2.base_pre
  37.3 0.7 copy-done.10
  38.0 0.4 convolution_add_fusion.base
  38.3 7.2 %all-to-all-done.1.incoming = bf16[32,16,512]{2,1,0:T(8,128)(2,1)S(1)} async-done(((bf16[32,16,512]{2,1,0:T(8,128)(2,1)}), bf16[32,16,512]{2,1,0:T(8,128)(2,1)S(1)}, u32[]{:S(2)}, u32[]{:S(2)}) %all-to-all-start.1) | async-done | bytes 524320 | tf_op jit(solution)/shard_map/all_to_all | solution.py:45
  45.6 0.0 copy-start.4
  45.6 0.0 copy-start.5
  45.6 2.3 %all_gather.12.hubs = bf16[512,512]{1,0:T(8,128)(2,1)S(1)} all-gather(bf16[256,512]{1,0:T(8,128)(2,1)S(1)} %slice_bitcast_fusion.2), channel_id=1, replica_groups=mesh['z'=8,'core'=2,'dom'=32] {'core'}, dimensions={0}, use_global_device_ids=true | all-gather | bytes 786432 | tf_op jit(solution)/shard_map/all_gather | solution.py:242
  48.0 0.1 broadcast_in_dim.11.inverse
  48.1 0.0 copy-done.6
  48.1 0.0 copy-done.7
  48.1 0.0 copy-done.4
  48.1 0.0 copy-done.5
  48.1 1.9 %middle.1 = (bf16[384,512]{1,0:T(8,128)(2,1)}, bf16[384,512]{1,0:T(8,128)(2,1)S(1)}, bf16[384,512]{1,0:T(8,128)(2,1)S(1)}) custom-call(bf16[512,512]{1,0:T(8,128)(2,1)S(1)} %all_gather.12.hubs, bf16[384,512]{1,0:T(8,128)(2,1)S(1)} %copy-done.6, bf16[32,16,512]{2,1,0:T(8,128)(2,1)S(1)} %all-to-all-done.1.incoming, bf16[384,256]{1,0:T(8,128)(2,1)S(1)} %copy-done.7, ...), custom_call_target="tpu_custom_call" | custom-call | flops 704643072 | bytes 5505024 | tf_op jit(solution)/shard_map/middle/pallas_call | solution.py:57
  50.0 0.0 copy-start.1
  50.0 0.0 copy-start.3
  50.0 0.0 copy-start.8
  50.0 2.5 %all_gather.15.both_means = bf16[768,512]{1,0:T(8,128)(2,1)S(1)} all-gather(bf16[384,512]{1,0:T(8,128)(2,1)S(1)} %get-tuple-element.16.grad_mean), channel_id=1, replica_groups=mesh['z'=8,'core'=2,'dom'=32] {'core'}, dimensions={0}, use_global_device_ids=true | all-gather | bytes 1179648 | tf_op jit(solution)/shard_map/all_gather | solution.py:268
  52.5 0.0 copy-done.1
  52.5 0.0 copy-done.3
  52.5 0.0 copy-done.8
  52.5 1.3 %pack.1 = bf16[32,16,512]{2,1,0:T(8,128)(2,1)} custom-call(bf16[256,384]{1,0:T(8,128)(2,1)S(1)} %copy-done.8, bf16[384,512]{1,0:T(8,128)(2,1)S(1)} %get-tuple-element.16.grad_mean, bf16[2,256,384]{2,1,0:T(8,128)(2,1)S(1)} %copy-done.3, bf16[768,512]{1,0:T(8,128)(2,1)S(1)} %all_gather.15.both_means, bf16[384,512]{1,0:T(8,128)(2,1)S(1)} %get-tuple-element.18.grad_pre), custom_call_target="tpu_custom_call" | custom-call | flops 301989888 | bytes 2686976 | tf_op jit(solution)/shard_map/pack/pallas_call | solution.py:57
  53.9 9.0 %all-to-all-start.2 = ((bf16[32,16,512]{2,1,0:T(8,128)(2,1)}), bf16[32,16,512]{2,1,0:T(8,128)(2,1)S(1)}, u32[]{:S(2)}, u32[]{:S(2)}) async-start(bf16[32,16,512]{2,1,0:T(8,128)(2,1)} %pack.1), calls=%async_computation.2 | async-start | bytes 1048576 | tf_op jit(solution)/shard_map/all_to_all | solution.py:45
  62.8 0.0 copy-start.2
  62.8 0.1 copy.25
  62.9 0.1 eq.45
  63.0 0.1 fusion.1.pick
  63.1 0.7 copy-done.2
  63.8 0.4 convolution_add_fusion.1
  64.2 0.7 copy-done.11
  64.9 0.4 fusion.base
  65.3 11.0 %all-to-all-done.2.returned = bf16[32,16,512]{2,1,0:T(8,128)(2,1)S(1)} async-done(((bf16[32,16,512]{2,1,0:T(8,128)(2,1)}), bf16[32,16,512]{2,1,0:T(8,128)(2,1)S(1)}, u32[]{:S(2)}, u32[]{:S(2)}) %all-to-all-start.2) | async-done | bytes 524320 | tf_op jit(solution)/shard_map/all_to_all | solution.py:45
  76.3 0.7 arrive.1
  76.9 7.2 %all-to-all-start.3 = ((f32[8,4,128]{2,1,0:T(4,128)}), f32[8,4,128]{2,1,0:T(4,128)S(1)}, u32[]{:S(2)}, u32[]{:S(2)}) async-start(f32[8,4,128]{2,1,0:T(4,128)} %arrive.1), calls=%async_computation.3 | async-start | bytes 32768 | tf_op jit(solution)/shard_map/all_to_all | solution.py:45
  84.1 0.1 broadcast_in_dim.24.at_hub
  84.3 0.4 tail.1.grad_local
  84.6 2.0 %all-to-all-done.3.parts = f32[8,4,128]{2,1,0:T(4,128)S(1)} async-done(((f32[8,4,128]{2,1,0:T(4,128)}), f32[8,4,128]{2,1,0:T(4,128)S(1)}, u32[]{:S(2)}, u32[]{:S(2)}) %all-to-all-start.3) | async-done | bytes 16416 | tf_op jit(solution)/shard_map/all_to_all | solution.py:45
  86.6 0.8 last.1
  (11 shorter events, 0.1 us)
Async XLA Ops:
  0.6 36.3 %copy-start = (bf16[512,512]{1,0:T(8,128)(2,1)S(1)}, bf16[512,512]{1,0:T(8,128)(2,1)}, u32[]{:S(2)}) copy-start(bf16[512,512]{1,0:T(8,128)(2,1)} %param.13) | copy-start | bytes 1572868
  0.6 17.2 %copy-start.9 = (bf16[384,512]{1,0:T(8,128)(2,1)S(1)}, bf16[384,512]{1,0:T(8,128)(2,1)}, u32[]{:S(2)}) copy-start(bf16[384,512]{1,0:T(8,128)(2,1)} %rows_ref.1) | copy-start | bytes 1179652
  2.7 18.3 %all-to-all-start = ((f32[8,4,128]{2,1,0:T(4,128)}), f32[8,4,128]{2,1,0:T(4,128)S(1)}, u32[]{:S(2)}, u32[]{:S(2)}) async-start(f32[8,4,128]{2,1,0:T(4,128)} %hub_row.1), calls=%async_computation | async-start | bytes 32768 | tf_op jit(solution)/shard_map/all_to_all | solution.py:45
  16.3 0.7 copy-start.16
  17.0 0.7 copy-start.13
  21.9 11.1 %copy-start.12 = (bf16[512,384]{1,0:T(8,128)(2,1)S(1)}, bf16[512,384]{1,0:T(8,128)(2,1)}, u32[]{:S(2)}) copy-start(bf16[512,384]{1,0:T(8,128)(2,1)} %get-tuple-element.17) | copy-start | bytes 1179652
  21.9 23.7 %all-to-all-start.1 = ((bf16[32,16,512]{2,1,0:T(8,128)(2,1)}), bf16[32,16,512]{2,1,0:T(8,128)(2,1)S(1)}, u32[]{:S(2)}, u32[]{:S(2)}) async-start(bf16[32,16,512]{2,1,0:T(8,128)(2,1)} %payload.1), calls=%async_computation.1 | async-start | bytes 1048576 | tf_op jit(solution)/shard_map/all_to_all | solution.py:45
  35.4 0.7 copy-start.15
  36.1 0.8 copy-start.14
  36.9 1.1 %copy-start.10 = (s32[384,384]{1,0:T(8,128)S(1)}, s32[384,384]{1,0:T(8,128)}, u32[]{:S(2)}) copy-start(s32[384,384]{1,0:T(8,128)} %param.17) | copy-start | bytes 1769476
  45.6 2.5 %copy-start.6 = (bf16[384,512]{1,0:T(8,128)(2,1)S(1)}, bf16[384,512]{1,0:T(8,128)(2,1)}, u32[]{:S(2)}) copy-start(bf16[384,512]{1,0:T(8,128)(2,1)} %get-tuple-element.12.hub_mat) | copy-start | bytes 1179652
  45.6 2.5 %copy-start.7 = (bf16[384,256]{1,0:T(8,128)(2,1)S(1)}, bf16[384,256]{1,0:T(8,128)(2,1)}, u32[]{:S(2)}) copy-start(bf16[384,256]{1,0:T(8,128)(2,1)} %get-tuple-element.13.remote_mat) | copy-start | bytes 589828
  45.6 2.5 %copy-start.4 = (bf16[512,512]{1,0:T(8,128)(2,1)S(1)}, bf16[512,512]{1,0:T(8,128)(2,1)}, u32[]{:S(2)}) copy-start(bf16[512,512]{1,0:T(8,128)(2,1)} %weight.1) | copy-start | bytes 1572868
  45.6 2.5 %copy-start.5 = (bf16[384,512]{1,0:T(8,128)(2,1)S(1)}, bf16[384,512]{1,0:T(8,128)(2,1)}, u32[]{:S(2)}) copy-start(bf16[384,512]{1,0:T(8,128)(2,1)} %grad.1) | copy-start | bytes 1179652
  50.0 2.5 %copy-start.1 = (bf16[384,512]{1,0:T(8,128)(2,1)}, bf16[384,512]{1,0:T(8,128)(2,1)S(1)}, u32[]{:S(2)}) copy-start(bf16[384,512]{1,0:T(8,128)(2,1)S(1)} %get-tuple-element.18.grad_pre) | copy-start | bytes 1179652
  50.0 2.5 %copy-start.3 = (bf16[2,256,384]{2,1,0:T(8,128)(2,1)S(1)}, bf16[2,256,384]{2,1,0:T(8,128)(2,1)}, u32[]{:S(2)}) copy-start(bf16[2,256,384]{2,1,0:T(8,128)(2,1)} %fusion.3.hub_t) | copy-start | bytes 1179652
  50.0 2.5 %copy-start.8 = (bf16[256,384]{1,0:T(8,128)(2,1)S(1)}, bf16[256,384]{1,0:T(8,128)(2,1)}, u32[]{:S(2)}) copy-start(bf16[256,384]{1,0:T(8,128)(2,1)} %get-tuple-element.15.remote_t) | copy-start | bytes 589828
  53.9 22.4 %all-to-all-start.2 = ((bf16[32,16,512]{2,1,0:T(8,128)(2,1)}), bf16[32,16,512]{2,1,0:T(8,128)(2,1)S(1)}, u32[]{:S(2)}, u32[]{:S(2)}) async-start(bf16[32,16,512]{2,1,0:T(8,128)(2,1)} %pack.1), calls=%async_computation.2 | async-start | bytes 1048576 | tf_op jit(solution)/shard_map/all_to_all | solution.py:45
  62.8 1.0 %copy-start.2 = (bf16[384,512]{1,0:T(8,128)(2,1)S(1)}, bf16[384,512]{1,0:T(8,128)(2,1)}, u32[]{:S(2)}) copy-start(bf16[384,512]{1,0:T(8,128)(2,1)} %copy-done.1) | copy-start | bytes 1179652
  63.8 1.1 %copy-start.11 = (s32[384,384]{1,0:T(8,128)S(1)}, s32[384,384]{1,0:T(8,128)}, u32[]{:S(2)}) copy-start(s32[384,384]{1,0:T(8,128)} %param.17) | copy-start | bytes 1769476
  76.9 9.7 %all-to-all-start.3 = ((f32[8,4,128]{2,1,0:T(4,128)}), f32[8,4,128]{2,1,0:T(4,128)S(1)}, u32[]{:S(2)}, u32[]{:S(2)}) async-start(f32[8,4,128]{2,1,0:T(4,128)} %arrive.1), calls=%async_computation.3 | async-start | bytes 32768 | tf_op jit(solution)/shard_map/all_to_all | solution.py:45

commit v5 on v4

--- a/solution.py
+++ b/solution.py
@@ -102,7 +102,8 @@
     )(hub_rows, features)
 
 
-def payload_kernel(along_z, outgoing, out_ref, held, sem):
+def payload_kernel(along_z, outgoing, base, base_pre, out_ref, held, sem):
+    del base, base_pre
     peers = out_ref.shape[0]
 
     def value(columns):
@@ -121,7 +122,7 @@
     shift = n_z.bit_length() - 1
 
     def source(place):
-        at_core, at_peer, at_z = place >> shift + 5, (place >> shift) & (PEERS - 1), (place + Z_ORDER[0]) & (n_z - 1)
+        at_core, at_peer, at_z = place >> shift + 5, (place >> shift) & (PEERS - 1), place & (n_z - 1)
         return (at_z * CORES + at_core) * PEERS + peer_at(at_peer)
 
     column = lax.broadcasted_iota(jnp.int32, (hubs, 1), 0)
@@ -176,7 +177,7 @@
 def arrive_kernel(returned, base, out_ref):
     del base
     total = jnp.sum(returned[...].astype(F32), axis=0)
-    out_ref[...] = split_lanes(total[total.shape[0] - out_ref.shape[0] :])
+    out_ref[...] = taken(split_lanes(total[total.shape[0] - out_ref.shape[0] :]), Z_ORDER)
 
 
 def tail_kernel(pick, returned, base, at_hub, out_ref):
@@ -222,19 +223,23 @@
     rows_f32 = jax.ShapeDtypeStruct((nodes, width), F32)
     rows_b16 = jax.ShapeDtypeStruct((nodes, width), BF16)
 
-    along_z = exchange(hub_row(hub_rows, features, n_z), "z", Z_ORDER)
+    along_z = exchange(hub_row(hub_rows, features, n_z), "z")
 
     live = jnp.arange(slots, dtype=jnp.int32)[None, :] < send_counts[0][:, None]
     picked = jnp.where(live, send_rows[0], -1)
     at_node = jnp.arange(nodes, dtype=jnp.int32)[:, None]
     pick = (picked.reshape(1, peers * slots) == at_node).astype(BF16)
     outgoing = transposed(pick, features).astype(BF16)
+    local_mat = local_adj.astype(BF16)
+    base = features.astype(F32) + matmul(local_mat, features)
+    base_pre = matmul(features, w_self) + bias_term
     (payload,) = in_vmem(
         payload_kernel,
         "payload",
         [jax.ShapeDtypeStruct((peers, block, width), BF16)],
-        (along_z, outgoing),
+        (along_z, outgoing, base, base_pre),
         flops=peers * block * width,
+        untouched=2,
         sent=(0,),
     )
     incoming = exchange(payload, "dom", PEER_ORDER)
@@ -251,10 +256,7 @@
     )
     chip_t = lax.all_gather(hub_t, "core", axis=0).reshape(n_core, n_core, half, nodes)
     chip_t = jnp.where(first_core, chip_t[:, 0], chip_t[:, 1])
-    local_mat = local_adj.astype(BF16)
-
-    base = features.astype(F32) + matmul(local_mat, features)
-    base_pre = matmul(features, w_self) + bias_term
+
     inverse = jnp.broadcast_to(1.0 / (degree.astype(F32)[:, None] + 1.0), (nodes, LANES))
     out_feats, grad_pre, grad_mean = in_vmem(
         middle_kernel,

time: 88.2 us -> 87.1 us (0.988)
  starting transfers between devices: 40.8 us -> 37.6 us
  local copies, waits for them, and re-layouts: 4.7 us -> 3.18 us
  waiting for transfers between devices: 20.2 us -> 21.7 us
  matrix products: 1.89 us -> 2.95 us
    all_to_all x4, starting transfers between devices: 40.8 us -> 37.6 us  [exchange(): lax.all_to_all(parts, axis, split_axis=0, concat_axis=0, tiled=True, axis...]
    all_to_all x4, waiting for transfers between devices: 20.2 us -> 21.7 us  [exchange(): lax.all_to_all(parts, axis, split_axis=0, concat_axis=0, tiled=True, axis...]
    unnamed x36 -> x30, local copies, waits for them, and re-layouts: 4.11 us -> 2.59 us
    dot_general x2, matrix products: 0.73 us -> 1.8 us  [matmul(): return jnp.dot(lhs, rhs, preferred_element_type=F32)]
  transfers between devices with their start and end apart: 4 -> 4, of which waited for: 3 -> 4; matrix products, arithmetic and copies ran while one was open for 4% -> 6% of each run, Pallas kernels for 4% -> 4%
where the time goes in v5:
time: 87.1 us; the launch traced here: 86.4 us
  starting transfers between devices  37.6 us (43%)
  waiting for transfers between devices  21.7 us (25%)
  Pallas kernels  10.1 us (12%)
  blocking collectives  7.51 us (9%)
  local copies, waits for them, and re-layouts  3.18 us (4%)
  matrix products  2.95 us (3%)
  other arithmetic  1.68 us (2%)
  between operations  1.62 us (2%)
    all_to_all x4, starting transfers between devices, exchange(): lax.all_to_all(parts, axis, split_axis=0, concat_axis=0, tiled=True, axis...  37.6 us
    all_to_all x4, waiting for transfers between devices, exchange(): lax.all_to_all(parts, axis, split_axis=0, concat_axis=0, tiled=True, axis...  21.7 us
    pallas_call x7, Pallas kernels, in_vmem(): pl.pallas_call(body, out_shape=shapes, in_specs=[spec] * (len(operands) -...  8.74 us
    all_gather x1, blocking collectives, on_device(): lax.all_gather(hub_t, 'core', axis=0).reshape(n_core, n_core, half, nodes)  2.7 us
    unnamed x30, local copies, waits for them, and re-layouts  2.59 us
    all_gather x1, blocking collectives, on_device(): both_means = lax.all_gather(grad_mean, 'core', axis=0, tiled=True)  2.5 us
    all_gather x1, blocking collectives, on_device(): all_hubs = lax.all_gather(same_core, 'core', axis=0, tiled=True)  2.31 us
    dot_general x2, matrix products, matmul(): return jnp.dot(lhs, rhs, preferred_element_type=F32)  1.8 us
  transfers between devices with their start and end apart: 4, of which 4 were waited for; matrix products, arithmetic and copies ran while one was open for 6% of the time, Pallas kernels for 4%

profile of v5, /device:TPU:8, one launch (start us, length us, event | category | flops | bytes accessed | tf_op | source)
XLA Modules:
  0.0 86.4 jit_solution(16397154586743053589)
XLA Ops:
  0.6 0.0 copy-start
  0.6 0.0 copy-start.8
  1.4 1.4 %hub_row.1 = f32[8,4,128]{2,1,0:T(4,128)} custom-call(s32[1,1]{1,0:T(1,128)} %copy.26.place_ref, bf16[384,512]{1,0:T(8,128)(2,1)} %rows_ref.1), custom_call_target="tpu_custom_call" | custom-call | tf_op jit(solution)/shard_map/hub_row/pallas_call | solution.py:94
  2.7 10.3 %all-to-all-start = ((f32[8,4,128]{2,1,0:T(4,128)}), f32[8,4,128]{2,1,0:T(4,128)S(1)}, u32[]{:S(2)}, u32[]{:S(2)}) async-start(f32[8,4,128]{2,1,0:T(4,128)} %hub_row.1), calls=%async_computation | async-start | bytes 32768 | tf_op jit(solution)/shard_map/all_to_all | solution.py:45
  13.1 0.0 copy-done.8
  13.1 1.4 %convolution_add_fusion.base = f32[384,512]{1,0:T(8,128)S(1)} fusion(bf16[384,512]{1,0:T(8,128)(2,1)S(1)} %copy-done.8, s32[384,384]{1,0:T(8,128)} %param.17), kind=kOutput, calls=%fused_computation | convolution fusion | flops 151535616 | bytes 1769472 | tf_op jit(solution)/shard_map/dot_general | solution.py:32
  14.5 0.0 copy-start.13
  14.5 0.6 copy-done.13
  15.2 0.0 copy-start.10
  15.2 0.1 copy.16
  15.3 0.1 lt.26
  15.4 0.5 copy-done.10
  15.9 0.1 copy.17
  15.9 0.0 copy-start.11
  15.9 0.1 squeeze.10
  16.0 0.0 copy-done
  16.0 0.6 copy-done.11
  16.6 0.4 convolution_add_fusion.2.base_pre
  17.0 0.4 convolution_convert_fusion.outgoing
  17.4 3.5 %all-to-all-done.along_z = f32[8,4,128]{2,1,0:T(4,128)S(1)} async-done(((f32[8,4,128]{2,1,0:T(4,128)}), f32[8,4,128]{2,1,0:T(4,128)S(1)}, u32[]{:S(2)}, u32[]{:S(2)}) %all-to-all-start) | async-done | bytes 16416 | tf_op jit(solution)/shard_map/all_to_all | solution.py:45
  20.8 0.9 %payload.1 = bf16[32,16,512]{2,1,0:T(8,128)(2,1)} custom-call(f32[8,4,128]{2,1,0:T(4,128)S(1)} %all-to-all-done.along_z, bf16[256,512]{1,0:T(8,128)(2,1)S(1)} %convolution_convert_fusion.outgoing, f32[384,512]{1,0:T(8,128)S(1)} %convolution_add_fusion.base, f32[384,512]{1,0:T(8,128)S(1)} %convolution_add_fusion.2.base_pre), custom_call_target="tpu_custom_call" | custom-call | flops 262144 | bytes 2375680 | tf_op jit(solution)/shard_map/payload/pallas_call | solution.py:57
  21.7 10.9 %all-to-all-start.1 = ((bf16[32,16,512]{2,1,0:T(8,128)(2,1)}), bf16[32,16,512]{2,1,0:T(8,128)(2,1)S(1)}, u32[]{:S(2)}, u32[]{:S(2)}) async-start(bf16[32,16,512]{2,1,0:T(8,128)(2,1)} %payload.1), calls=%async_computation.1 | async-start | bytes 1048576 | tf_op jit(solution)/shard_map/all_to_all | solution.py:45
  32.7 2.8 %adjacency.1 = (bf16[384,512]{1,0:T(8,128)(2,1)}, bf16[512,384]{1,0:T(8,128)(2,1)}, bf16[384,256]{1,0:T(8,128)(2,1)}, bf16[256,384]{1,0:T(8,128)(2,1)}) custom-call(s32[384,512]{1,0:T(8,128)} %hub_adj.1, s32[384,256]{1,0:T(8,128)} %remote_adj.1), custom_call_target="tpu_custom_call" | custom-call | tf_op jit(solution)/shard_map/adjacency/pallas_call | solution.py:57
  35.5 0.0 copy-start.12
  35.5 2.7 %all-gather = bf16[1024,384]{1,0:T(8,128)(2,1)S(1)} all-gather(bf16[512,384]{1,0:T(8,128)(2,1)} %get-tuple-element.17), channel_id=2, replica_groups=mesh['z'=8,'core'=2,'dom'=32] {'core'}, dimensions={0}, use_global_device_ids=true | all-gather | bytes 1179648 | tf_op jit(solution)/shard_map/all_gather | solution.py:257
  38.2 0.0 copy-done.12
  38.2 0.8 fusion.3.hub_t
  39.0 5.4 %all-to-all-done.1.incoming = bf16[32,16,512]{2,1,0:T(8,128)(2,1)S(1)} async-done(((bf16[32,16,512]{2,1,0:T(8,128)(2,1)}), bf16[32,16,512]{2,1,0:T(8,128)(2,1)S(1)}, u32[]{:S(2)}, u32[]{:S(2)}) %all-to-all-start.1) | async-done | bytes 524320 | tf_op jit(solution)/shard_map/all_to_all | solution.py:45
  44.4 0.0 copy-start.5
  44.4 0.0 copy-start.6
  44.4 0.0 copy-start.3
  44.4 0.0 copy-start.4
  44.4 2.3 %all_gather.12.hubs = bf16[512,512]{1,0:T(8,128)(2,1)S(1)} all-gather(bf16[256,512]{1,0:T(8,128)(2,1)S(1)} %slice_bitcast_fusion.2), channel_id=1, replica_groups=mesh['z'=8,'core'=2,'dom'=32] {'core'}, dimensions={0}, use_global_device_ids=true | all-gather | bytes 786432 | tf_op jit(solution)/shard_map/all_gather | solution.py:247
  46.7 0.1 broadcast_in_dim.11.inverse
  46.9 0.0 copy-done.5
  46.9 0.0 copy-done.6
  46.9 0.0 copy-done.3
  46.9 0.0 copy-done.4
  46.9 1.9 %middle.1 = (bf16[384,512]{1,0:T(8,128)(2,1)}, bf16[384,512]{1,0:T(8,128)(2,1)S(1)}, bf16[384,512]{1,0:T(8,128)(2,1)S(1)}) custom-call(bf16[512,512]{1,0:T(8,128)(2,1)S(1)} %all_gather.12.hubs, bf16[384,512]{1,0:T(8,128)(2,1)S(1)} %copy-done.5, bf16[32,16,512]{2,1,0:T(8,128)(2,1)S(1)} %all-to-all-done.1.incoming, bf16[384,256]{1,0:T(8,128)(2,1)S(1)} %copy-done.6, ...), custom_call_target="tpu_custom_call" | custom-call | flops 704643072 | bytes 5505024 | tf_op jit(solution)/shard_map/middle/pallas_call | solution.py:57
  48.8 0.0 copy-start.2
  48.8 0.0 copy-start.7
  48.8 2.5 %all_gather.15.both_means = bf16[768,512]{1,0:T(8,128)(2,1)S(1)} all-gather(bf16[384,512]{1,0:T(8,128)(2,1)S(1)} %get-tuple-element.16.grad_mean), channel_id=1, replica_groups=mesh['z'=8,'core'=2,'dom'=32] {'core'}, dimensions={0}, use_global_device_ids=true | all-gather | bytes 1179648 | tf_op jit(solution)/shard_map/all_gather | solution.py:270
  51.3 0.0 copy-done.2
  51.3 0.0 copy-done.7
  51.3 1.3 %pack.1 = bf16[32,16,512]{2,1,0:T(8,128)(2,1)} custom-call(bf16[256,384]{1,0:T(8,128)(2,1)S(1)} %copy-done.7, bf16[384,512]{1,0:T(8,128)(2,1)S(1)} %get-tuple-element.16.grad_mean, bf16[2,256,384]{2,1,0:T(8,128)(2,1)S(1)} %copy-done.2, bf16[768,512]{1,0:T(8,128)(2,1)S(1)} %all_gather.15.both_means, bf16[384,512]{1,0:T(8,128)(2,1)S(1)} %get-tuple-element.18.grad_pre), custom_call_target="tpu_custom_call" | custom-call | flops 301989888 | bytes 2686976 | tf_op jit(solution)/shard_map/pack/pallas_call | solution.py:57
  52.6 9.1 %all-to-all-start.2 = ((bf16[32,16,512]{2,1,0:T(8,128)(2,1)}), bf16[32,16,512]{2,1,0:T(8,128)(2,1)S(1)}, u32[]{:S(2)}, u32[]{:S(2)}) async-start(bf16[32,16,512]{2,1,0:T(8,128)(2,1)} %pack.1), calls=%async_computation.2 | async-start | bytes 1048576 | tf_op jit(solution)/shard_map/all_to_all | solution.py:45
  61.8 0.1 copy.25
  61.9 0.1 eq.45
  61.9 0.8 fusion.1.pick
  62.8 0.0 copy-start.9
  62.8 0.4 convolution_add_fusion.1
  63.2 0.7 copy-done.9
  63.8 0.4 fusion.base
  64.3 10.9 %all-to-all-done.2.returned = bf16[32,16,512]{2,1,0:T(8,128)(2,1)S(1)} async-done(((bf16[32,16,512]{2,1,0:T(8,128)(2,1)}), bf16[32,16,512]{2,1,0:T(8,128)(2,1)S(1)}, u32[]{:S(2)}, u32[]{:S(2)}) %all-to-all-start.2) | async-done | bytes 524320 | tf_op jit(solution)/shard_map/all_to_all | solution.py:45
  75.2 0.0 copy-start.1
  75.2 0.6 arrive.1
  75.9 7.2 %all-to-all-start.3 = ((f32[8,4,128]{2,1,0:T(4,128)}), f32[8,4,128]{2,1,0:T(4,128)S(1)}, u32[]{:S(2)}, u32[]{:S(2)}) async-start(f32[8,4,128]{2,1,0:T(4,128)} %arrive.1), calls=%async_computation.3 | async-start | bytes 32768 | tf_op jit(solution)/shard_map/all_to_all | solution.py:45
  83.1 0.1 broadcast_in_dim.24.at_hub
  83.2 0.0 copy-done.1
  83.2 0.4 tail.1.grad_local
  83.6 2.0 %all-to-all-done.3.parts = f32[8,4,128]{2,1,0:T(4,128)S(1)} async-done(((f32[8,4,128]{2,1,0:T(4,128)}), f32[8,4,128]{2,1,0:T(4,128)S(1)}, u32[]{:S(2)}, u32[]{:S(2)}) %all-to-all-start.3) | async-done | bytes 16416 | tf_op jit(solution)/shard_map/all_to_all | solution.py:45
  85.5 0.8 last.1
  (7 shorter events, 0.1 us)
Async XLA Ops:
  0.6 15.4 %copy-start = (bf16[512,512]{1,0:T(8,128)(2,1)S(1)}, bf16[512,512]{1,0:T(8,128)(2,1)}, u32[]{:S(2)}) copy-start(bf16[512,512]{1,0:T(8,128)(2,1)} %param.13) | copy-start | bytes 1572868
  0.6 12.4 %copy-start.8 = (bf16[384,512]{1,0:T(8,128)(2,1)S(1)}, bf16[384,512]{1,0:T(8,128)(2,1)}, u32[]{:S(2)}) copy-start(bf16[384,512]{1,0:T(8,128)(2,1)} %rows_ref.1) | copy-start | bytes 1179652
  2.7 18.1 %all-to-all-start = ((f32[8,4,128]{2,1,0:T(4,128)}), f32[8,4,128]{2,1,0:T(4,128)S(1)}, u32[]{:S(2)}, u32[]{:S(2)}) async-start(f32[8,4,128]{2,1,0:T(4,128)} %hub_row.1), calls=%async_computation | async-start | bytes 32768 | tf_op jit(solution)/shard_map/all_to_all | solution.py:45
  14.5 0.7 copy-start.13
  15.2 0.7 copy-start.10
  15.9 0.7 copy-start.11
  21.7 22.7 %all-to-all-start.1 = ((bf16[32,16,512]{2,1,0:T(8,128)(2,1)}), bf16[32,16,512]{2,1,0:T(8,128)(2,1)S(1)}, u32[]{:S(2)}, u32[]{:S(2)}) async-start(bf16[32,16,512]{2,1,0:T(8,128)(2,1)} %payload.1), calls=%async_computation.1 | async-start | bytes 1048576 | tf_op jit(solution)/shard_map/all_to_all | solution.py:45
  35.5 2.7 %copy-start.12 = (s32[384]{0:T(512)S(1)}, s32[384]{0:T(512)}, u32[]{:S(2)}) copy-start(s32[384]{0:T(512)} %param.16) | copy-start | bytes 4612
  44.4 2.5 %copy-start.5 = (bf16[384,512]{1,0:T(8,128)(2,1)S(1)}, bf16[384,512]{1,0:T(8,128)(2,1)}, u32[]{:S(2)}) copy-start(bf16[384,512]{1,0:T(8,128)(2,1)} %get-tuple-element.12.hub_mat) | copy-start | bytes 1179652
  44.4 2.5 %copy-start.6 = (bf16[384,256]{1,0:T(8,128)(2,1)S(1)}, bf16[384,256]{1,0:T(8,128)(2,1)}, u32[]{:S(2)}) copy-start(bf16[384,256]{1,0:T(8,128)(2,1)} %get-tuple-element.13.remote_mat) | copy-start | bytes 589828
  44.4 2.5 %copy-start.3 = (bf16[512,512]{1,0:T(8,128)(2,1)S(1)}, bf16[512,512]{1,0:T(8,128)(2,1)}, u32[]{:S(2)}) copy-start(bf16[512,512]{1,0:T(8,128)(2,1)} %weight.1) | copy-start | bytes 1572868
  44.4 2.5 %copy-start.4 = (bf16[384,512]{1,0:T(8,128)(2,1)S(1)}, bf16[384,512]{1,0:T(8,128)(2,1)}, u32[]{:S(2)}) copy-start(bf16[384,512]{1,0:T(8,128)(2,1)} %grad.1) | copy-start | bytes 1179652
  48.8 2.5 %copy-start.2 = (bf16[2,256,384]{2,1,0:T(8,128)(2,1)S(1)}, bf16[2,256,384]{2,1,0:T(8,128)(2,1)}, u32[]{:S(2)}) copy-start(bf16[2,256,384]{2,1,0:T(8,128)(2,1)} %fusion.3.hub_t) | copy-start | bytes 1179652
  48.8 2.5 %copy-start.7 = (bf16[256,384]{1,0:T(8,128)(2,1)S(1)}, bf16[256,384]{1,0:T(8,128)(2,1)}, u32[]{:S(2)}) copy-start(bf16[256,384]{1,0:T(8,128)(2,1)} %get-tuple-element.15.remote_t) | copy-start | bytes 589828
  52.6 22.6 %all-to-all-start.2 = ((bf16[32,16,512]{2,1,0:T(8,128)(2,1)}), bf16[32,16,512]{2,1,0:T(8,128)(2,1)S(1)}, u32[]{:S(2)}, u32[]{:S(2)}) async-start(bf16[32,16,512]{2,1,0:T(8,128)(2,1)} %pack.1), calls=%async_computation.2 | async-start | bytes 1048576 | tf_op jit(solution)/shard_map/all_to_all | solution.py:45
  62.8 1.1 %copy-start.9 = (s32[384,384]{1,0:T(8,128)S(1)}, s32[384,384]{1,0:T(8,128)}, u32[]{:S(2)}) copy-start(s32[384,384]{1,0:T(8,128)} %param.17) | copy-start | bytes 1769476
  75.2 8.0 %copy-start.1 = (bf16[384,512]{1,0:T(8,128)(2,1)S(1)}, bf16[384,512]{1,0:T(8,128)(2,1)}, u32[]{:S(2)}) copy-start(bf16[384,512]{1,0:T(8,128)(2,1)} %fusion.1.pick) | copy-start | bytes 1179652
  75.9 9.7 %all-to-all-start.3 = ((f32[8,4,128]{2,1,0:T(4,128)}), f32[8,4,128]{2,1,0:T(4,128)S(1)}, u32[]{:S(2)}, u32[]{:S(2)}) async-start(f32[8,4,128]{2,1,0:T(4,128)} %arrive.1), calls=%async_computation.3 | async-start | bytes 32768 | tf_op jit(solution)/shard_map/all_to_all | solution.py:45

commit v6 on v5

--- a/solution.py
+++ b/solution.py
@@ -15,7 +15,7 @@
 
 
 def peer_at(place):
-    place = (place + 18) & (PEERS - 1)
+    place = (place + 19) & (PEERS - 1)
     return ((place & 3) << 3) | (place >> 2)
 
 

time: 87.1 us -> 86.8 us (level)
  no operation moved by 1% of the time
where the time goes in v6:
time: 86.8 us; the launch traced here: 86.1 us
  starting transfers between devices  37.6 us (43%)
  waiting for transfers between devices  21.5 us (25%)
  Pallas kernels  10.1 us (12%)
  blocking collectives  7.51 us (9%)
  local copies, waits for them, and re-layouts  3.19 us (4%)
  matrix products  2.95 us (3%)
  other arithmetic  1.68 us (2%)
  between operations  1.62 us (2%)
    all_to_all x4, starting transfers between devices, exchange(): lax.all_to_all(parts, axis, split_axis=0, concat_axis=0, tiled=True, axis...  37.6 us
    all_to_all x4, waiting for transfers between devices, exchange(): lax.all_to_all(parts, axis, split_axis=0, concat_axis=0, tiled=True, axis...  21.5 us
    pallas_call x7, Pallas kernels, in_vmem(): pl.pallas_call(body, out_shape=shapes, in_specs=[spec] * (len(operands) -...  8.73 us
    all_gather x1, blocking collectives, on_device(): lax.all_gather(hub_t, 'core', axis=0).reshape(n_core, n_core, half, nodes)  2.7 us
    unnamed x30, local copies, waits for them, and re-layouts  2.59 us
    all_gather x1, blocking collectives, on_device(): both_means = lax.all_gather(grad_mean, 'core', axis=0, tiled=True)  2.5 us
    all_gather x1, blocking collectives, on_device(): all_hubs = lax.all_gather(same_core, 'core', axis=0, tiled=True)  2.31 us
    dot_general x2, matrix products, matmul(): return jnp.dot(lhs, rhs, preferred_element_type=F32)  1.8 us
  transfers between devices with their start and end apart: 4, of which 4 were waited for; matrix products, arithmetic and copies ran while one was open for 6% of the time, Pallas kernels for 4%

profile of v6, /device:TPU:8, one launch (start us, length us, event | category | flops | bytes accessed | tf_op | source)
XLA Modules:
  0.0 86.1 jit_solution(1942176588443889617)
XLA Ops:
  0.6 0.0 copy-start
  0.6 0.0 copy-start.8
  1.4 1.4 %hub_row.1 = f32[8,4,128]{2,1,0:T(4,128)} custom-call(s32[1,1]{1,0:T(1,128)} %copy.26.place_ref, bf16[384,512]{1,0:T(8,128)(2,1)} %rows_ref.1), custom_call_target="tpu_custom_call" | custom-call | tf_op jit(solution)/shard_map/hub_row/pallas_call | solution.py:94
  2.7 10.3 %all-to-all-start = ((f32[8,4,128]{2,1,0:T(4,128)}), f32[8,4,128]{2,1,0:T(4,128)S(1)}, u32[]{:S(2)}, u32[]{:S(2)}) async-start(f32[8,4,128]{2,1,0:T(4,128)} %hub_row.1), calls=%async_computation | async-start | bytes 32768 | tf_op jit(solution)/shard_map/all_to_all | solution.py:45
  13.1 0.0 copy-done.8
  13.1 1.4 %convolution_add_fusion.base = f32[384,512]{1,0:T(8,128)S(1)} fusion(bf16[384,512]{1,0:T(8,128)(2,1)S(1)} %copy-done.8, s32[384,384]{1,0:T(8,128)} %param.17), kind=kOutput, calls=%fused_computation | convolution fusion | flops 151535616 | bytes 1769472 | tf_op jit(solution)/shard_map/dot_general | solution.py:32
  14.5 0.0 copy-start.13
  14.5 0.6 copy-done.13
  15.2 0.0 copy-start.10
  15.2 0.1 copy.16
  15.3 0.1 lt.26
  15.4 0.5 copy-done.10
  15.9 0.1 copy.17
  15.9 0.0 copy-start.11
  15.9 0.1 squeeze.10
  16.0 0.0 copy-done
  16.0 0.6 copy-done.11
  16.6 0.4 convolution_add_fusion.2.base_pre
  17.0 0.4 convolution_convert_fusion.outgoing
  17.4 3.5 %all-to-all-done.along_z = f32[8,4,128]{2,1,0:T(4,128)S(1)} async-done(((f32[8,4,128]{2,1,0:T(4,128)}), f32[8,4,128]{2,1,0:T(4,128)S(1)}, u32[]{:S(2)}, u32[]{:S(2)}) %all-to-all-start) | async-done | bytes 16416 | tf_op jit(solution)/shard_map/all_to_all | solution.py:45
  20.8 0.9 %payload.1 = bf16[32,16,512]{2,1,0:T(8,128)(2,1)} custom-call(f32[8,4,128]{2,1,0:T(4,128)S(1)} %all-to-all-done.along_z, bf16[256,512]{1,0:T(8,128)(2,1)S(1)} %convolution_convert_fusion.outgoing, f32[384,512]{1,0:T(8,128)S(1)} %convolution_add_fusion.base, f32[384,512]{1,0:T(8,128)S(1)} %convolution_add_fusion.2.base_pre), custom_call_target="tpu_custom_call" | custom-call | flops 262144 | bytes 2375680 | tf_op jit(solution)/shard_map/payload/pallas_call | solution.py:57
  21.7 10.7 %all-to-all-start.1 = ((bf16[32,16,512]{2,1,0:T(8,128)(2,1)}), bf16[32,16,512]{2,1,0:T(8,128)(2,1)S(1)}, u32[]{:S(2)}, u32[]{:S(2)}) async-start(bf16[32,16,512]{2,1,0:T(8,128)(2,1)} %payload.1), calls=%async_computation.1 | async-start | bytes 1048576 | tf_op jit(solution)/shard_map/all_to_all | solution.py:45
  32.4 2.8 %adjacency.1 = (bf16[384,512]{1,0:T(8,128)(2,1)}, bf16[512,384]{1,0:T(8,128)(2,1)}, bf16[384,256]{1,0:T(8,128)(2,1)}, bf16[256,384]{1,0:T(8,128)(2,1)}) custom-call(s32[384,512]{1,0:T(8,128)} %hub_adj.1, s32[384,256]{1,0:T(8,128)} %remote_adj.1), custom_call_target="tpu_custom_call" | custom-call | tf_op jit(solution)/shard_map/adjacency/pallas_call | solution.py:57
  35.2 0.0 copy-start.12
  35.2 2.7 %all-gather = bf16[1024,384]{1,0:T(8,128)(2,1)S(1)} all-gather(bf16[512,384]{1,0:T(8,128)(2,1)} %get-tuple-element.17), channel_id=2, replica_groups=mesh['z'=8,'core'=2,'dom'=32] {'core'}, dimensions={0}, use_global_device_ids=true | all-gather | bytes 1179648 | tf_op jit(solution)/shard_map/all_gather | solution.py:257
  37.9 0.0 copy-done.12
  37.9 0.8 fusion.3.hub_t
  38.7 5.4 %all-to-all-done.1.incoming = bf16[32,16,512]{2,1,0:T(8,128)(2,1)S(1)} async-done(((bf16[32,16,512]{2,1,0:T(8,128)(2,1)}), bf16[32,16,512]{2,1,0:T(8,128)(2,1)S(1)}, u32[]{:S(2)}, u32[]{:S(2)}) %all-to-all-start.1) | async-done | bytes 524320 | tf_op jit(solution)/shard_map/all_to_all | solution.py:45
  44.1 0.0 copy-start.5
  44.1 0.0 copy-start.6
  44.1 0.0 copy-start.3
  44.1 0.0 copy-start.4
  44.2 2.3 %all_gather.12.hubs = bf16[512,512]{1,0:T(8,128)(2,1)S(1)} all-gather(bf16[256,512]{1,0:T(8,128)(2,1)S(1)} %slice_bitcast_fusion.2), channel_id=1, replica_groups=mesh['z'=8,'core'=2,'dom'=32] {'core'}, dimensions={0}, use_global_device_ids=true | all-gather | bytes 786432 | tf_op jit(solution)/shard_map/all_gather | solution.py:247
  46.5 0.1 broadcast_in_dim.11.inverse
  46.6 0.0 copy-done.5
  46.6 0.0 copy-done.6
  46.6 0.0 copy-done.3
  46.6 0.0 copy-done.4
  46.6 1.9 %middle.1 = (bf16[384,512]{1,0:T(8,128)(2,1)}, bf16[384,512]{1,0:T(8,128)(2,1)S(1)}, bf16[384,512]{1,0:T(8,128)(2,1)S(1)}) custom-call(bf16[512,512]{1,0:T(8,128)(2,1)S(1)} %all_gather.12.hubs, bf16[384,512]{1,0:T(8,128)(2,1)S(1)} %copy-done.5, bf16[32,16,512]{2,1,0:T(8,128)(2,1)S(1)} %all-to-all-done.1.incoming, bf16[384,256]{1,0:T(8,128)(2,1)S(1)} %copy-done.6, ...), custom_call_target="tpu_custom_call" | custom-call | flops 704643072 | bytes 5505024 | tf_op jit(solution)/shard_map/middle/pallas_call | solution.py:57
  48.5 0.0 copy-start.2
  48.5 0.0 copy-start.7
  48.5 2.5 %all_gather.15.both_means = bf16[768,512]{1,0:T(8,128)(2,1)S(1)} all-gather(bf16[384,512]{1,0:T(8,128)(2,1)S(1)} %get-tuple-element.16.grad_mean), channel_id=1, replica_groups=mesh['z'=8,'core'=2,'dom'=32] {'core'}, dimensions={0}, use_global_device_ids=true | all-gather | bytes 1179648 | tf_op jit(solution)/shard_map/all_gather | solution.py:270
  51.0 0.0 copy-done.2
  51.0 0.0 copy-done.7
  51.0 1.3 %pack.1 = bf16[32,16,512]{2,1,0:T(8,128)(2,1)} custom-call(bf16[256,384]{1,0:T(8,128)(2,1)S(1)} %copy-done.7, bf16[384,512]{1,0:T(8,128)(2,1)S(1)} %get-tuple-element.16.grad_mean, bf16[2,256,384]{2,1,0:T(8,128)(2,1)S(1)} %copy-done.2, bf16[768,512]{1,0:T(8,128)(2,1)S(1)} %all_gather.15.both_means, bf16[384,512]{1,0:T(8,128)(2,1)S(1)} %get-tuple-element.18.grad_pre), custom_call_target="tpu_custom_call" | custom-call | flops 301989888 | bytes 2686976 | tf_op jit(solution)/shard_map/pack/pallas_call | solution.py:57
  52.4 9.4 %all-to-all-start.2 = ((bf16[32,16,512]{2,1,0:T(8,128)(2,1)}), bf16[32,16,512]{2,1,0:T(8,128)(2,1)S(1)}, u32[]{:S(2)}, u32[]{:S(2)}) async-start(bf16[32,16,512]{2,1,0:T(8,128)(2,1)} %pack.1), calls=%async_computation.2 | async-start | bytes 1048576 | tf_op jit(solution)/shard_map/all_to_all | solution.py:45
  61.8 0.1 copy.25
  61.9 0.1 eq.45
  61.9 0.8 fusion.1.pick
  62.8 0.0 copy-start.9
  62.8 0.4 convolution_add_fusion.1
  63.2 0.7 copy-done.9
  63.9 0.4 fusion.base
  64.3 10.7 %all-to-all-done.2.returned = bf16[32,16,512]{2,1,0:T(8,128)(2,1)S(1)} async-done(((bf16[32,16,512]{2,1,0:T(8,128)(2,1)}), bf16[32,16,512]{2,1,0:T(8,128)(2,1)S(1)}, u32[]{:S(2)}, u32[]{:S(2)}) %all-to-all-start.2) | async-done | bytes 524320 | tf_op jit(solution)/shard_map/all_to_all | solution.py:45
  75.0 0.0 copy-start.1
  75.0 0.6 arrive.1
  75.6 7.2 %all-to-all-start.3 = ((f32[8,4,128]{2,1,0:T(4,128)}), f32[8,4,128]{2,1,0:T(4,128)S(1)}, u32[]{:S(2)}, u32[]{:S(2)}) async-start(f32[8,4,128]{2,1,0:T(4,128)} %arrive.1), calls=%async_computation.3 | async-start | bytes 32768 | tf_op jit(solution)/shard_map/all_to_all | solution.py:45
  82.8 0.1 broadcast_in_dim.24.at_hub
  83.0 0.0 copy-done.1
  83.0 0.4 tail.1.grad_local
  83.3 2.0 %all-to-all-done.3.parts = f32[8,4,128]{2,1,0:T(4,128)S(1)} async-done(((f32[8,4,128]{2,1,0:T(4,128)}), f32[8,4,128]{2,1,0:T(4,128)S(1)}, u32[]{:S(2)}, u32[]{:S(2)}) %all-to-all-start.3) | async-done | bytes 16416 | tf_op jit(solution)/shard_map/all_to_all | solution.py:45
  85.3 0.8 last.1
  (7 shorter events, 0.1 us)
Async XLA Ops:
  0.6 15.4 %copy-start = (bf16[512,512]{1,0:T(8,128)(2,1)S(1)}, bf16[512,512]{1,0:T(8,128)(2,1)}, u32[]{:S(2)}) copy-start(bf16[512,512]{1,0:T(8,128)(2,1)} %param.13) | copy-start | bytes 1572868
  0.6 12.4 %copy-start.8 = (bf16[384,512]{1,0:T(8,128)(2,1)S(1)}, bf16[384,512]{1,0:T(8,128)(2,1)}, u32[]{:S(2)}) copy-start(bf16[384,512]{1,0:T(8,128)(2,1)} %rows_ref.1) | copy-start | bytes 1179652
  2.7 18.1 %all-to-all-start = ((f32[8,4,128]{2,1,0:T(4,128)}), f32[8,4,128]{2,1,0:T(4,128)S(1)}, u32[]{:S(2)}, u32[]{:S(2)}) async-start(f32[8,4,128]{2,1,0:T(4,128)} %hub_row.1), calls=%async_computation | async-start | bytes 32768 | tf_op jit(solution)/shard_map/all_to_all | solution.py:45
  14.5 0.7 copy-start.13
  15.2 0.7 copy-start.10
  15.9 0.7 copy-start.11
  21.7 22.4 %all-to-all-start.1 = ((bf16[32,16,512]{2,1,0:T(8,128)(2,1)}), bf16[32,16,512]{2,1,0:T(8,128)(2,1)S(1)}, u32[]{:S(2)}, u32[]{:S(2)}) async-start(bf16[32,16,512]{2,1,0:T(8,128)(2,1)} %payload.1), calls=%async_computation.1 | async-start | bytes 1048576 | tf_op jit(solution)/shard_map/all_to_all | solution.py:45
  35.2 2.7 %copy-start.12 = (s32[384]{0:T(512)S(1)}, s32[384]{0:T(512)}, u32[]{:S(2)}) copy-start(s32[384]{0:T(512)} %param.16) | copy-start | bytes 4612
  44.1 2.5 %copy-start.5 = (bf16[384,512]{1,0:T(8,128)(2,1)S(1)}, bf16[384,512]{1,0:T(8,128)(2,1)}, u32[]{:S(2)}) copy-start(bf16[384,512]{1,0:T(8,128)(2,1)} %get-tuple-element.12.hub_mat) | copy-start | bytes 1179652
  44.1 2.5 %copy-start.6 = (bf16[384,256]{1,0:T(8,128)(2,1)S(1)}, bf16[384,256]{1,0:T(8,128)(2,1)}, u32[]{:S(2)}) copy-start(bf16[384,256]{1,0:T(8,128)(2,1)} %get-tuple-element.13.remote_mat) | copy-start | bytes 589828
  44.1 2.5 %copy-start.3 = (bf16[512,512]{1,0:T(8,128)(2,1)S(1)}, bf16[512,512]{1,0:T(8,128)(2,1)}, u32[]{:S(2)}) copy-start(bf16[512,512]{1,0:T(8,128)(2,1)} %weight.1) | copy-start | bytes 1572868
  44.1 2.5 %copy-start.4 = (bf16[384,512]{1,0:T(8,128)(2,1)S(1)}, bf16[384,512]{1,0:T(8,128)(2,1)}, u32[]{:S(2)}) copy-start(bf16[384,512]{1,0:T(8,128)(2,1)} %grad.1) | copy-start | bytes 1179652
  48.5 2.5 %copy-start.2 = (bf16[2,256,384]{2,1,0:T(8,128)(2,1)S(1)}, bf16[2,256,384]{2,1,0:T(8,128)(2,1)}, u32[]{:S(2)}) copy-start(bf16[2,256,384]{2,1,0:T(8,128)(2,1)} %fusion.3.hub_t) | copy-start | bytes 1179652
  48.5 2.5 %copy-start.7 = (bf16[256,384]{1,0:T(8,128)(2,1)S(1)}, bf16[256,384]{1,0:T(8,128)(2,1)}, u32[]{:S(2)}) copy-start(bf16[256,384]{1,0:T(8,128)(2,1)} %get-tuple-element.15.remote_t) | copy-start | bytes 589828
  52.4 22.6 %all-to-all-start.2 = ((bf16[32,16,512]{2,1,0:T(8,128)(2,1)}), bf16[32,16,512]{2,1,0:T(8,128)(2,1)S(1)}, u32[]{:S(2)}, u32[]{:S(2)}) async-start(bf16[32,16,512]{2,1,0:T(8,128)(2,1)} %pack.1), calls=%async_computation.2 | async-start | bytes 1048576 | tf_op jit(solution)/shard_map/all_to_all | solution.py:45
  62.8 1.1 %copy-start.9 = (s32[384,384]{1,0:T(8,128)S(1)}, s32[384,384]{1,0:T(8,128)}, u32[]{:S(2)}) copy-start(s32[384,384]{1,0:T(8,128)} %param.17) | copy-start | bytes 1769476
  75.0 8.0 %copy-start.1 = (bf16[384,512]{1,0:T(8,128)(2,1)S(1)}, bf16[384,512]{1,0:T(8,128)(2,1)}, u32[]{:S(2)}) copy-start(bf16[384,512]{1,0:T(8,128)(2,1)} %fusion.1.pick) | copy-start | bytes 1179652
  75.6 9.7 %all-to-all-start.3 = ((f32[8,4,128]{2,1,0:T(4,128)}), f32[8,4,128]{2,1,0:T(4,128)S(1)}, u32[]{:S(2)}, u32[]{:S(2)}) async-start(f32[8,4,128]{2,1,0:T(4,128)} %arrive.1), calls=%async_computation.3 | async-start | bytes 32768 | tf_op jit(solution)/shard_map/all_to_all | solution.py:45
